TPU v7x, 32 devices: a whole 2x2x4 slice. The times are simulated.
32 devices in a mesh: blocks: 2 (over x), rows: 8 (over z, y), pairs: 2 (over core).
Axes of the slice: x: 2, y: 2, z: 4, core: 2. Of those that a mesh axis runs over, the one named last changes fastest.
Arguments:
- interferograms: bfloat16 [2, 1500, 256, 256], P(None, 'pairs', ('blocks', 'rows')), parts along dimension 2, may hold values from -6 to 6
- pair_dates: int32 [1500, 2], replicated, may hold values from 0 to 299, as said below
- mask_table: int32 [4, 1500], replicated, may hold values 0 or 1
- gap_dates: int32 [4, 30], replicated, may hold values from 0 to 299, as said below
- pattern_ids: int32 [256, 256], P(('blocks', 'rows')), parts along dimension 0, may hold values from 0 to 3
Outputs:
- corrected: float32 [256, 300, 256], P(('blocks', 'rows', 'pairs')), parts along dimension 0
There are 2 independent parts, one for each index of `blocks`. A program takes and returns all parts, laid end to end along the dimension named above; an argument that names none is the same for every part. Nothing has to cross between parts.
Inputs may be any that keep to these rules, and one draw needn't show every extreme that they name: `pair_dates`: row k holds the earlier and the later date of pair k; the later exceeds the earlier by 1 to 5. `gap_dates`: each row lists 30 different dates. `pattern_ids`: each pixel belongs to one of 4 gap pattern classes.
All inputs are finite; a program needn't handle non-finite values.
Results may differ from a plain program's by a relative error of at most 0.0044.
Values may be sent and summed in bfloat16 or wider, within the bound.
A program may use at most 192 MiB of HBM per device.

v0:
```python
import jax
import jax.numpy as jnp
from jax import lax
from jax.sharding import PartitionSpec as P

DATES = 300
NPAT = 4
RADIUS = 6


damping = 0.5
corr_length = 10.0
gauss_width = 2.0


def extended_2(value, sides, width):
    for axis, dim in sides:
        count, length = (lax.axis_size(axis), value.shape[dim])
        up = [(i, (i + 1) % count) for i in range(count - 1)]
        down = [(j, i) for i, j in up]
        last = lax.slice_in_dim(value, length - width, length, axis=dim)
        leading = lax.slice_in_dim(value, 0, width, axis=dim)
        before = lax.ppermute(last, axis, up)
        after = lax.ppermute(leading, axis, down)
        value = jnp.concatenate([before, value, after], axis=dim)
    return value


def build_operators(pair_dates, mask_rows, gap_rows):
    dates = jnp.arange(DATES, dtype=jnp.int32)
    first_hot = (dates[None, :] == pair_dates[:, 0:1]).astype(jnp.float32)
    second_hot = (dates[None, :] == pair_dates[:, 1:2]).astype(jnp.float32)
    incidence = second_hot - first_hot
    gapped = jnp.any(gap_rows[:, :, None] == dates[None, None, :], axis=1).astype(jnp.float32)
    lag = jnp.abs(dates[:, None] - dates[None, :]).astype(jnp.float32)
    cov = jnp.exp(-lag / corr_length)
    ident = jnp.eye(DATES, dtype=jnp.float32)
    hp = lax.Precision.HIGHEST

    def single(args):
        valid_row, gap_row = args
        gap_first = jnp.dot(first_hot, gap_row, precision=hp)
        gap_second = jnp.dot(second_hot, gap_row, precision=hp)
        keep = valid_row.astype(jnp.float32) * (1.0 - gap_first) * (1.0 - gap_second)
        weighted = incidence * keep[:, None]
        normal = jnp.dot(weighted.T, incidence, precision=hp) + damping * ident
        factor = jnp.linalg.cholesky(normal)
        solved = jax.scipy.linalg.cho_solve((factor, True), weighted.T)
        observed = 1.0 - gap_row
        masked = cov * observed[:, None] * observed[None, :] + jnp.diag(gap_row)
        cross = cov * observed[:, None] * gap_row[None, :]
        factor_two = jnp.linalg.cholesky(masked)
        weights = jax.scipy.linalg.cho_solve((factor_two, True), cross)
        return solved + jnp.dot(weights.T, solved, precision=hp)

    return lax.map(single, (mask_rows, gapped)).astype(jnp.bfloat16)


def gauss_kernel():
    spots = jnp.arange(-RADIUS, RADIUS + 1, dtype=jnp.float32)
    raw = jnp.exp(-spots * spots / (2.0 * gauss_width * gauss_width))
    return raw / jnp.sum(raw)


def select_class(by_class, classes_here):
    labels = jnp.arange(by_class.shape[1], dtype=jnp.int32)
    hit = classes_here[:, None, None, :] == labels[None, :, None, None]
    return jnp.sum(jnp.where(hit, by_class, 0.0), axis=1)


def body(interferograms, pair_dates, mask_table, gap_dates, pattern_ids):
    strip = interferograms.shape[2]
    columns = interferograms.shape[3]
    my_rows = strip // lax.axis_size("pairs")
    extended = extended_2(interferograms, (("rows", 2),), 2)
    planes = extended.astype(jnp.float32)
    along = sum((planes[:, :, offset : offset + strip, :] for offset in range(5)))
    widened = jnp.pad(along, ((0, 0), (0, 0), (0, 0), (2, 2)))
    boxed = sum((widened[:, :, :, offset : offset + columns] for offset in range(5)))
    modulus = jnp.sqrt(boxed[0] * boxed[0] + boxed[1] * boxed[1])
    looks = (boxed[1] / jnp.maximum(modulus, 1.0)).astype(jnp.bfloat16)
    share = NPAT // lax.axis_size("pairs")
    begin = lax.axis_index("pairs") * share
    mask_mine = lax.dynamic_slice_in_dim(mask_table, begin, share, 0)
    gaps_mine = lax.dynamic_slice_in_dim(gap_dates, begin, share, 0)
    mine = build_operators(pair_dates, mask_mine, gaps_mine)
    operators = lax.all_gather(mine, "pairs", axis=0, tiled=True)
    classes_here = lax.dynamic_slice_in_dim(
        pattern_ids, lax.axis_index("pairs") * my_rows, my_rows, 0
    )
    by_class = jnp.einsum(
        "qtk,krc->rqtc",
        operators,
        lax.all_to_all(looks, "pairs", split_axis=1, concat_axis=0, tiled=True),
        preferred_element_type=jnp.float32,
    )
    series = select_class(by_class, classes_here)
    kernel = gauss_kernel()
    rimmed = extended_2(series.astype(jnp.bfloat16), ((("rows", "pairs"), 0),), RADIUS).astype(
        series.dtype
    )
    smooth_rows = sum(
        (kernel[offset] * rimmed[offset : offset + my_rows] for offset in range(2 * RADIUS + 1))
    )
    padded = jnp.pad(smooth_rows, ((0, 0), (0, 0), (RADIUS, RADIUS)))
    screen = sum(
        (
            kernel[offset] * padded[:, :, offset : offset + columns]
            for offset in range(2 * RADIUS + 1)
        )
    )
    return series - screen


def solution(mesh):
    placed = (
        P(None, "pairs", ("blocks", "rows"), None),
        P(),
        P(),
        P(),
        P(("blocks", "rows"), None),
    )
    return jax.shard_map(
        body,
        mesh=mesh,
        in_specs=placed,
        out_specs=P(("blocks", "rows", "pairs"), None, None),
        check_vma=False,
    )
```

profile of v0, /device:TPU:1, one launch (start us, length us, event | category | flops | bytes accessed | tf_op | source)
XLA Modules:
  0.0 773.9 jit_solution(16684866653949220057)
XLA Ops:
  6.5 7.9 %fusion.163 = (bf16[2,750,2,256]{3,2,1,0:T(2,128)(2,1)}, bf16[2,750,2,256]{3,2,1,0:T(2,128)(2,1)}) fusion(bf16[2,750,16,256]{3,2,1,0:T(8,128)(2,1)} %param.8), kind=kLoop, calls=%fused_computation.272 | loop fusion | bytes 6144000 | tf_op jit(solution)/shard_map/slice | solution.py:21
  15.8 5.8 collective-permute-start
  22.3 507.6 %while.22 = (s32[]{:T(128)}, bf16[2,300,1500]{2,0,1:T(2,128)(2,1)}, s32[2,1500]{1,0:T(2,128)}, f32[2,300]{1,0:T(2,128)S(1)}, s32[1500]{0:T(1024)S(1)}, /*index=5...) while((s32[]{:T(128)}, bf16[2,300,1500]{2,0,1:T(2,128)(2,1)}, ...), condition=%wide.region_8.10_spmd.clone.clone, body=%wide.region_1.9_spmd.clone.clone.sunk | while | flops 6125674496 | bytes 50542120 | solution.py:56
  29.9 11.7 %cholesky.659 = f32[128,128]{1,0:T(8,128)S(1)} custom-call(f32[128,128]{1,0:T(8,128)S(1)} %copy.176), custom_call_target="Cholesky" | custom-call | tf_op jit(solution)/shard_map/while/body/eval_jaxpr/jit(cholesky)/cholesky | solution.py:52
  42.2 9.8 %custom-call.45 = f32[1,128,128]{1,2,0:T(8,128)S(1)} custom-call(f32[1,128,128]{2,1,0:T(8,128)S(1)} %get-tuple-element.333), custom_call_target="InvertDiagBlocksLowerTriangular" | custom-call | tf_op jit(solution)/shard_map/while/body/eval_jaxpr/jit(cholesky)/cholesky | solution.py:52
  52.8 11.9 %cholesky.662 = f32[128,128]{1,0:T(8,128)S(1)} custom-call(f32[128,128]{1,0:T(8,128)S(1)} %copy.177), custom_call_target="Cholesky" | custom-call | tf_op jit(solution)/shard_map/while/body/eval_jaxpr/jit(cholesky)/cholesky | solution.py:52
  65.3 9.8 %custom-call.46 = f32[1,128,128]{1,2,0:T(8,128)S(1)} custom-call(f32[1,128,128]{2,1,0:T(8,128)S(1)} %get-tuple-element.337), custom_call_target="InvertDiagBlocksLowerTriangular" | custom-call | tf_op jit(solution)/shard_map/while/body/eval_jaxpr/jit(cholesky)/cholesky | solution.py:52
  75.7 4.0 cholesky.663
  84.4 5.5 fusion.298
  90.9 12.2 %cholesky.667 = f32[128,128]{1,0:T(8,128)S(1)} custom-call(f32[128,128]{1,0:T(8,128)S(1)} %cholesky.666), custom_call_target="Cholesky" | custom-call | tf_op jit(solution)/shard_map/while/body/eval_jaxpr/jit(cholesky)/cholesky | solution.py:47
  103.2 9.8 %custom-call.47 = f32[1,128,128]{1,2,0:T(8,128)S(1)} custom-call(f32[1,128,128]{2,1,0:T(8,128)S(1)} %get-tuple-element.344), custom_call_target="InvertDiagBlocksLowerTriangular" | custom-call | tf_op jit(solution)/shard_map/while/body/eval_jaxpr/jit(cholesky)/cholesky | solution.py:47
  115.3 11.7 %cholesky.670 = f32[128,128]{1,0:T(8,128)S(1)} custom-call(f32[128,128]{1,0:T(8,128)S(1)} %cholesky.669), custom_call_target="Cholesky" | custom-call | tf_op jit(solution)/shard_map/while/body/eval_jaxpr/jit(cholesky)/cholesky | solution.py:47
  127.0 9.8 %custom-call.48 = f32[1,128,128]{1,2,0:T(8,128)S(1)} custom-call(f32[1,128,128]{2,1,0:T(8,128)S(1)} %get-tuple-element.348), custom_call_target="InvertDiagBlocksLowerTriangular" | custom-call | tf_op jit(solution)/shard_map/while/body/eval_jaxpr/jit(cholesky)/cholesky | solution.py:47
  137.9 4.2 cholesky.671
  150.3 30.3 %custom-call.49 = f32[3,128,128]{1,2,0:T(8,128)S(1)} custom-call(f32[3,128,128]{2,1,0:T(8,128)} %pad_maximum_fusion.4), custom_call_target="InvertDiagBlocksLowerTriangular" | custom-call | tf_op jit(solution)/shard_map/while/body/eval_jaxpr/jit(_cho_solve)/triangular_solve | solution.py:48
  195.0 5.7 while.24
  200.7 29.7 %custom-call.50 = f32[3,128,128]{1,2,0:T(8,128)S(1)} custom-call(f32[3,128,128]{2,1,0:T(8,128)S(1)} %pad_maximum_fusion.5), custom_call_target="InvertDiagBlocksLowerTriangular" | custom-call | tf_op jit(solution)/shard_map/while/body/eval_jaxpr/jit(_cho_solve)/triangular_solve | solution.py:53
  237.5 5.6 fusion.313
  245.4 27.0 %dynamic_update_slice.7 = bf16[2,300,1500]{2,0,1:T(2,128)(2,1)} dynamic-update-slice(bf16[2,300,1500]{2,0,1:T(2,128)(2,1)} %get-tuple-element.415, bf16[1,300,1500]{2,0,1:T(2,128)(2,1)S(1)} %copy.182, s32[]{:T(128)S(6)} %copy.208, s32[]{:T(128)} %constant.175.clone.1..sunk, s32[]{:T(128)} %constant.175.clone.1..sunk) | dynamic-update-slice | bytes 1800004 | tf_op jit(solution)/shard_map/while/body/jit(dynamic_update_index_in_dim)/dynamic_update_slice | solution.py:56
  280.2 11.7 %cholesky.659 = f32[128,128]{1,0:T(8,128)S(1)} custom-call(f32[128,128]{1,0:T(8,128)S(1)} %copy.176), custom_call_target="Cholesky" | custom-call | tf_op jit(solution)/shard_map/while/body/eval_jaxpr/jit(cholesky)/cholesky | solution.py:52
  292.5 9.8 %custom-call.45 = f32[1,128,128]{1,2,0:T(8,128)S(1)} custom-call(f32[1,128,128]{2,1,0:T(8,128)S(1)} %get-tuple-element.333), custom_call_target="InvertDiagBlocksLowerTriangular" | custom-call | tf_op jit(solution)/shard_map/while/body/eval_jaxpr/jit(cholesky)/cholesky | solution.py:52
  303.1 11.9 %cholesky.662 = f32[128,128]{1,0:T(8,128)S(1)} custom-call(f32[128,128]{1,0:T(8,128)S(1)} %copy.177), custom_call_target="Cholesky" | custom-call | tf_op jit(solution)/shard_map/while/body/eval_jaxpr/jit(cholesky)/cholesky | solution.py:52
  315.6 9.8 %custom-call.46 = f32[1,128,128]{1,2,0:T(8,128)S(1)} custom-call(f32[1,128,128]{2,1,0:T(8,128)S(1)} %get-tuple-element.337), custom_call_target="InvertDiagBlocksLowerTriangular" | custom-call | tf_op jit(solution)/shard_map/while/body/eval_jaxpr/jit(cholesky)/cholesky | solution.py:52
  326.0 4.0 cholesky.663
  334.7 5.5 fusion.298
  341.2 12.1 %cholesky.667 = f32[128,128]{1,0:T(8,128)S(1)} custom-call(f32[128,128]{1,0:T(8,128)S(1)} %cholesky.666), custom_call_target="Cholesky" | custom-call | tf_op jit(solution)/shard_map/while/body/eval_jaxpr/jit(cholesky)/cholesky | solution.py:47
  353.4 9.8 %custom-call.47 = f32[1,128,128]{1,2,0:T(8,128)S(1)} custom-call(f32[1,128,128]{2,1,0:T(8,128)S(1)} %get-tuple-element.344), custom_call_target="InvertDiagBlocksLowerTriangular" | custom-call | tf_op jit(solution)/shard_map/while/body/eval_jaxpr/jit(cholesky)/cholesky | solution.py:47
  365.5 11.7 %cholesky.670 = f32[128,128]{1,0:T(8,128)S(1)} custom-call(f32[128,128]{1,0:T(8,128)S(1)} %cholesky.669), custom_call_target="Cholesky" | custom-call | tf_op jit(solution)/shard_map/while/body/eval_jaxpr/jit(cholesky)/cholesky | solution.py:47
  377.2 9.8 %custom-call.48 = f32[1,128,128]{1,2,0:T(8,128)S(1)} custom-call(f32[1,128,128]{2,1,0:T(8,128)S(1)} %get-tuple-element.348), custom_call_target="InvertDiagBlocksLowerTriangular" | custom-call | tf_op jit(solution)/shard_map/while/body/eval_jaxpr/jit(cholesky)/cholesky | solution.py:47
  388.2 4.2 cholesky.671
  400.5 30.3 %custom-call.49 = f32[3,128,128]{1,2,0:T(8,128)S(1)} custom-call(f32[3,128,128]{2,1,0:T(8,128)} %pad_maximum_fusion.4), custom_call_target="InvertDiagBlocksLowerTriangular" | custom-call | tf_op jit(solution)/shard_map/while/body/eval_jaxpr/jit(_cho_solve)/triangular_solve | solution.py:48
  445.2 5.7 while.24
  450.9 29.7 %custom-call.50 = f32[3,128,128]{1,2,0:T(8,128)S(1)} custom-call(f32[3,128,128]{2,1,0:T(8,128)S(1)} %pad_maximum_fusion.5), custom_call_target="InvertDiagBlocksLowerTriangular" | custom-call | tf_op jit(solution)/shard_map/while/body/eval_jaxpr/jit(_cho_solve)/triangular_solve | solution.py:53
  487.7 5.6 fusion.313
  495.6 27.0 %dynamic_update_slice.7 = bf16[2,300,1500]{2,0,1:T(2,128)(2,1)} dynamic-update-slice(bf16[2,300,1500]{2,0,1:T(2,128)(2,1)} %get-tuple-element.415, bf16[1,300,1500]{2,0,1:T(2,128)(2,1)S(1)} %copy.182, s32[]{:T(128)S(6)} %copy.208, s32[]{:T(128)} %constant.175.clone.1..sunk, s32[]{:T(128)} %constant.175.clone.1..sunk) | dynamic-update-slice | bytes 1800004 | tf_op jit(solution)/shard_map/while/body/jit(dynamic_update_index_in_dim)/dynamic_update_slice | solution.py:56
  532.9 12.3 %copy.139 = bf16[2,750,16,256]{3,1,2,0:T(8,128)(2,1)} copy(bf16[2,750,16,256]{3,2,1,0:T(8,128)(2,1)} %param.8) | data formatting | bytes 24576000 | tf_op args[0]
  548.4 16.6 %maximum_convert_fusion = f32[2,750,20,256]{3,1,2,0:T(8,128)} fusion(bf16[2,750,2,256]{3,1,2,0:T(8,128)(2,1)S(1)} %copy.140, bf16[2,750,16,256]{3,1,2,0:T(8,128)(2,1)} %copy.139, bf16[2,750,2,256]{3,1,2,0:T(8,128)(2,1)S(1)} %copy.138), kind=kLoop, calls=%fused_computation.180 | loop fusion | flops 23040000 | bytes 46080000 | tf_op jit(solution)/shard_map/convert_element_type | solution.py:76
  565.0 47.4 %slice_add_fusion = f32[2,750,16,256]{3,1,2,0:T(8,128)} fusion(f32[2,750,20,256]{3,1,2,0:T(8,128)} %maximum_convert_fusion), kind=kLoop, calls=%fused_computation.176 | loop fusion | flops 24576000 | bytes 147456000 | tf_op jit(solution)/shard_map/add | solution.py:77
  612.4 59.4 %fusion.107 = f32[2,750,16,256]{3,1,2,0:T(8,128)} fusion(f32[2,750,16,256]{3,1,2,0:T(8,128)} %slice_add_fusion), kind=kLoop, calls=%fused_computation.175 | loop fusion | flops 24576000 | bytes 49152000 | tf_op jit(solution)/shard_map/add | solution.py:79
  671.7 10.5 %fusion.113 = bf16[750,16,256]{2,0,1:T(8,128)(2,1)S(1)} fusion(f32[2,750,16,256]{3,1,2,0:T(8,128)} %fusion.107), kind=kLoop, calls=%fused_computation.188 | loop fusion | flops 18432000 | bytes 30720000 | tf_op jit(solution)/shard_map/convert_element_type | solution.py:81
  682.3 9.6 %all_to_all.18 = bf16[750,16,256]{2,0,1:T(8,128)(2,1)S(1)} all-to-all(bf16[750,16,256]{2,0,1:T(8,128)(2,1)S(1)} %fusion.113), channel_id=1, replica_groups=mesh['blocks'=2,'rows'=8,'pairs'=2] {'pairs'}, dimensions={1} | all-to-all | bytes 12288000 | tf_op jit(solution)/shard_map/all_to_all | solution.py:94
  691.8 5.0 copy.142
  696.8 11.5 %fusion.114 = f32[8,300,256]{2,1,0:T(8,128)S(1)} fusion(pred[8,4,256]{2,1,0:T(4,128)(4,1)S(1)} %iota_compare_fusion.15, bf16[1500,8,256,1]{2,1,0,3:T(8,128)(2,1)} %bitcast.228, bf16[4,300,1500]{2,1,0:T(8,128)(2,1)} %all-gather.2.cloned.1.call-done), kind=kOutput, calls=%fused_computation.190 | convolution fusion | flops 7377100800 | bytes 12209792 | tf_op jit(solution)/shard_map/qtk,krc->rqtc/dot_general | solution.py:91
  716.5 7.1 collective-permute-done.3
  723.5 10.5 %collective-permute-done.2 = bf16[6,300,256]{2,1,0:T(8,128)(2,1)S(1)} collective-permute-done((bf16[6,300,256]{2,1,0:T(8,128)(2,1)S(1)}, bf16[6,300,256]{2,1,0:T(8,128)(2,1)S(1)}, u32[]{:S(2)}, u32[]{:S(2)}) %collective-permute-start.2) | collective-permute-done | bytes 921632 | tf_op jit(solution)/shard_map/ppermute | solution.py:23
  734.5 10.6 %fusion.145 = f32[8,300,256]{2,1,0:T(8,128)S(1)} fusion(f32[20,300,256]{2,1,0:T(8,128)S(1)} %maximum_convert_fusion.1, f32[]{:T(128)} %bitcast.21, f32[]{:T(128)} %bitcast.20, f32[]{:T(128)} %bitcast.19, f32[]{:T(128)} %bitcast.18, f32[]{:T(128)} %bitcast.17, f32[]{:T(128)} %bitcast.16, f32[]{:T(128)} %bitcast.15, f32[]{:T(128)} %bitcast.14, f32[]{:T(128)} %bitcast.13, ...), kind=kLoop, calls=%fused_computation.233 | loop fusion | flops 15360000 | bytes 34406452 | tf_op jit(solution)/shard_map/add | solution.py:102
  745.1 17.1 %fusion.133 = f32[8,300,256]{2,1,0:T(8,128)} fusion(f32[8,300,256]{2,1,0:T(8,128)S(1)} %fusion.114, f32[8,300,256]{2,1,0:T(8,128)S(1)} %fusion.145, f32[]{:T(128)} %bitcast.21, f32[]{:T(128)} %bitcast.20, f32[]{:T(128)} %bitcast.19, f32[]{:T(128)} %bitcast.18, f32[]{:T(128)} %bitcast.17, f32[]{:T(128)} %bitcast.16, f32[]{:T(128)} %bitcast.15, f32[]{:T(128)} %bitcast.14, ...), kind=kLoop, calls=%fused_computation.220 | loop fusion | flops 15974400 | bytes 7372852 | tf_op jit(solution)/shard_map/sub | solution.py:112
  762.2 4.6 copy.146
  (239 shorter events, 129.5 us)
Async XLA Ops:
  6.5 15.0 %copy-start = (s32[4,1500]{1,0:T(4,128)S(1)}, s32[4,1500]{1,0:T(4,128)}, u32[]{:S(2)}) copy-start(s32[4,1500]{1,0:T(4,128)} %param.10) | copy-start | bytes 72004
  6.5 15.6 %copy-start.11 = (s32[4,30]{1,0:T(4,128)S(1)}, s32[4,30]{1,0:T(4,128)}, u32[]{:S(2)}) copy-start(s32[4,30]{1,0:T(4,128)} %param.11) | copy-start | bytes 1444
  6.5 15.7 %copy-start.9 = (s32[1500,2]{0,1:T(2,128)S(1)}, s32[1500,2]{0,1:T(2,128)}, u32[]{:S(2)}) copy-start(s32[1500,2]{0,1:T(2,128)} %param.9) | copy-start | bytes 36004
  6.5 690.3 %all-gather.2.cloned.1.call-start = ((), (), s32[]{:S(2)}) async-start(), calls=%async_computation.1 | async-start | bytes 5603328 | tf_op jit(solution)/shard_map/all_gather | solution.py:87
  14.5 530.7 %collective-permute-start.1 = (bf16[2,750,2,256]{3,2,1,0:T(2,128)(2,1)}, bf16[2,750,2,256]{3,2,1,0:T(2,128)(2,1)}, u32[]{:S(2)}, u32[]{:S(2)}) collective-permute-start(bf16[2,750,2,256]{3,2,1,0:T(2,128)(2,1)} %get-tuple-element.185), channel_id=1, source_target_pairs={{2,0},{4,2},{6,4},{8,6},{10,8},{12,10},{14,12},{3,1},{5,3},{7,5},{... | collective-permute-start | bytes 4608008 | tf_op jit(solution)/shard_map/ppermute | solution.py:24
  15.8 531.0 %collective-permute-start = (bf16[2,750,2,256]{3,2,1,0:T(2,128)(2,1)}, bf16[2,750,2,256]{3,2,1,0:T(2,128)(2,1)}, u32[]{:S(2)}, u32[]{:S(2)}) collective-permute-start(bf16[2,750,2,256]{3,2,1,0:T(2,128)(2,1)} %get-tuple-element.184), channel_id=1, source_target_pairs={{0,2},{2,4},{4,6},{6,8},{8,10},{10,12},{12,14},{1,3},{3,5},{5,7},{... | collective-permute-start | bytes 4608008 | tf_op jit(solution)/shard_map/ppermute | solution.py:23
  22.5 6.9 copy-start.7
  83.6 0.8 copy-start.4
  90.1 0.8 copy-start.6
  149.4 0.9 copy-start.3
  183.8 2.2 copy-start.2
  193.3 37.1 %copy-start.5 = (f32[300,300]{1,0:T(8,128)S(1)}, f32[300,300]{1,0:T(8,128)}, u32[]{:S(2)}) copy-start(f32[300,300]{1,0:T(8,128)} %get-tuple-element.357) | copy-start | bytes 1080004 | tf_op jit(solution)/shard_map/while
  245.4 27.0 %copy-start.8 = (f32[2,300]{1,0:T(2,128)S(1)}, f32[2,300]{1,0:T(2,128)}, u32[]{:S(2)}) copy-start(f32[2,300]{1,0:T(2,128)} %copy-done.7) | copy-start | bytes 7204 | tf_op jit(solution)/shard_map/while
  272.8 6.9 copy-start.7
  333.8 0.8 copy-start.4
  340.4 0.8 copy-start.6
  399.6 0.9 copy-start.3
  434.0 2.2 copy-start.2
  443.5 37.1 %copy-start.5 = (f32[300,300]{1,0:T(8,128)S(1)}, f32[300,300]{1,0:T(8,128)}, u32[]{:S(2)}) copy-start(f32[300,300]{1,0:T(8,128)} %get-tuple-element.357) | copy-start | bytes 1080004 | tf_op jit(solution)/shard_map/while
  495.6 27.0 %copy-start.8 = (f32[2,300]{1,0:T(2,128)S(1)}, f32[2,300]{1,0:T(2,128)}, u32[]{:S(2)}) copy-start(f32[2,300]{1,0:T(2,128)} %copy-done.7) | copy-start | bytes 7204 | tf_op jit(solution)/shard_map/while
  532.8 12.3 %copy-start.10 = (s32[16,256]{1,0:T(8,128)S(1)}, s32[16,256]{1,0:T(8,128)}, u32[]{:S(2)}) copy-start(s32[16,256]{1,0:T(8,128)} %param.12) | copy-start | bytes 49156
  708.6 14.9 %collective-permute-start.3 = (bf16[6,300,256]{2,1,0:T(8,128)(2,1)S(1)}, bf16[6,300,256]{2,1,0:T(8,128)(2,1)S(1)}, u32[]{:S(2)}, u32[]{:S(2)}) collective-permute-start(bf16[6,300,256]{2,1,0:T(8,128)(2,1)S(1)} %get-tuple-element.187), channel_id=1, source_target_pairs={{1,0},{2,1},{3,2},{4,3},{5,4},{6,5},{7,6},{8,7},{9,8},{10,9},{11,1... | collective-permute-start | bytes 2764808 | tf_op jit(solution)/shard_map/ppermute | solution.py:24
  710.9 23.1 %collective-permute-start.2 = (bf16[6,300,256]{2,1,0:T(8,128)(2,1)S(1)}, bf16[6,300,256]{2,1,0:T(8,128)(2,1)S(1)}, u32[]{:S(2)}, u32[]{:S(2)}) collective-permute-start(bf16[6,300,256]{2,1,0:T(8,128)(2,1)S(1)} %get-tuple-element.186), channel_id=1, source_target_pairs={{0,1},{1,2},{2,3},{3,4},{4,5},{5,6},{6,7},{7,8},{8,9},{9,10},{10,1... | collective-permute-start | bytes 2764808 | tf_op jit(solution)/shard_map/ppermute | solution.py:23
  745.1 21.7 %copy-start.1 = (s32[4,1500]{1,0:T(4,128)S(1)}, s32[4,1500]{1,0:T(4,128)}, u32[]{:S(2)}) copy-start(s32[4,1500]{1,0:T(4,128)} %param.10) | copy-start | bytes 72004
Sparse Core Ops, SparseCore 0:
  533.0 14.4 all-gather.1
where the time goes:
time: 784 us; the launch traced here: 774 us
  other arithmetic  490 us (62%)
  local copies, waits for them, and re-layouts  121 us (15%)
  matrix products  93.3 us (12%)
  waiting for transfers between devices  17.6 us (2%)
  loops' own time  16.6 us (2%)
  between operations  13.8 us (2%)
  starting transfers between devices  12.6 us (2%)
  blocking collectives  9.55 us (1%)
    another operation x20, other arithmetic, single(): factor_two = jnp.linalg.cholesky(masked)  101 us
    another operation x20, other arithmetic, single(): factor = jnp.linalg.cholesky(normal)  98 us
    another operation x12, other arithmetic, single(): solved = jax.scipy.linalg.cho_solve((factor, True), weighted.T)  62.2 us
    another operation x8, other arithmetic, single(): weights = jax.scipy.linalg.cho_solve((factor_two, True), cross)  59.7 us
    add x1, other arithmetic, body(): sum((widened[:, :, :, offset:offset + columns] for offset in range(5)))  59.4 us
    dynamic_update_slice x4, local copies, waits for them, and re-layouts, build_operators(): return lax.map(single, (mask_rows, gapped)).astype(jnp.bfloat16)  58.5 us
    add x1, other arithmetic, body(): along = sum((planes[:, :, offset:offset + strip, :] for offset in range(5)))  47.4 us
    another operation x20, matrix products, single(): solved = jax.scipy.linalg.cho_solve((factor, True), weighted.T)  28 us
  transfers between devices with their start and end apart: 5, of which 2 were waited for; matrix products, arithmetic and copies ran while one was open for 84% of the time, Pallas kernels for 0%

commit v1 on v0

v1 whole, which is shorter than its diff:
```python
import functools

import jax
import ml_dtypes
import numpy as np
import jax.numpy as jnp
from jax import lax
from jax.experimental import pallas as pl
from jax.experimental.pallas import tpu as pltpu
from jax.sharding import PartitionSpec as P

DATES = 300
NPAT = 4
SPAN = 5
RADIUS = 6
LANES = 128
BLOCKS = DATES // SPAN
BLOCKS_PAD = 64
DATES_PAD = 304
LEVELS = 6
RIM = 32


damping = 0.5
corr_length = 10.0
gauss_width = 2.0


def round_up(value, unit):
    return -(-value // unit) * unit


def block_matmul(left, right, transposed=False):
    size = len(left)
    out = []
    for a in range(size):
        row = []
        for b in range(size):
            total = None
            for m in range(size):
                term = left[a][m] * (right[b][m] if transposed else right[m][b])
                total = term if total is None else total + term
            row.append(total)
        out.append(row)
    return out


def block_inverse(matrix):
    size = len(matrix)
    work = [list(row) for row in matrix]
    for k in range(size):
        pivot = 1.0 / work[k][k]
        work[k] = [pivot if j == k else work[k][j] * pivot for j in range(size)]
        for i in range(size):
            if i != k:
                factor = work[i][k]
                work[i] = [
                    -factor * pivot if j == k else work[i][j] - factor * work[k][j]
                    for j in range(size)
                ]
    return work


def moved(blocks, shift):
    return [[pltpu.roll(item, shift % LANES, 1) for item in row] for row in blocks]


def reduction_kernel(keep_ref, early_ref, late_ref, coef_ref):
    early = early_ref[...]
    span = late_ref[...] - early
    keep = keep_ref[...]
    classes = keep.shape[0]
    picked = jnp.concatenate(
        [jnp.where(span == d, keep, 0.0) for d in range(1, SPAN + 1)], axis=0
    ).astype(jnp.bfloat16)
    count = {}
    for a in range(SPAN):
        date = SPAN * lax.broadcasted_iota(jnp.int32, (LANES, early.shape[1]), 0) + a
        hot = jnp.where(date == early, 1.0, 0.0).astype(jnp.bfloat16)
        counts = lax.dot_general(
            picked, hot, (((1,), (1,)), ((), ())), preferred_element_type=jnp.float32
        )
        for d in range(1, SPAN + 1):
            count[d, a] = counts[(d - 1) * classes : d * classes]
    diagonal, upper = [], []
    for a in range(SPAN):
        total = damping
        for d in range(1, SPAN + 1):
            total = total + count[d, a]
            if a >= d:
                total = total + count[d, a - d]
            else:
                total = total + pltpu.roll(count[d, a - d + SPAN], 1, 1)
        diagonal.append(
            [total if b == a else -count[abs(b - a), min(a, b)] for b in range(SPAN)]
        )
        zero = jnp.zeros_like(total)
        upper.append([-count[SPAN + b - a, a] if b <= a else zero for b in range(SPAN)])
    slot = 0
    step = 1
    while step < BLOCKS:
        inverse = block_inverse(diagonal)
        flipped = [list(row) for row in zip(*upper)]
        below = block_matmul(flipped, inverse)
        gamma = [[-x for x in row] for row in block_matmul(upper, moved(inverse, -step))]
        alpha = [[-x for x in row] for row in moved(below, step)]
        first = moved(block_matmul(below, upper), step)
        second = block_matmul(gamma, upper, transposed=True)
        diagonal = [
            [diagonal[a][b] - first[a][b] + second[a][b] for b in range(SPAN)]
            for a in range(SPAN)
        ]
        upper = block_matmul(gamma, moved(upper, -step))
        for part in (alpha, gamma):
            for row in part:
                for item in row:
                    coef_ref[slot] = item
                    slot += 1
        step *= 2
    for row in block_inverse(diagonal):
        for item in row:
            coef_ref[slot] = item
            slot += 1


def inverse_kernel(coef_ref, mix_ref, high_ref, mid_ref, low_ref, state_ref, flat_ref):
    tile = pl.program_id(1)
    state_ref[...] = jnp.zeros_like(state_ref)
    column = lax.broadcasted_iota(jnp.int32, (BLOCKS_PAD, LANES), 1) + tile * LANES
    date = SPAN * lax.broadcasted_iota(jnp.int32, (BLOCKS_PAD, LANES), 0)
    for a in range(SPAN):
        state_ref[a, RIM : RIM + BLOCKS_PAD] = jnp.where(date + a == column, 1.0, 0.0)
    coef = coef_ref[0]
    slot = 0
    step = 1
    while step < BLOCKS:
        before = [state_ref[b, RIM - step : RIM - step + BLOCKS_PAD] for b in range(SPAN)]
        after = [state_ref[b, RIM + step : RIM + step + BLOCKS_PAD] for b in range(SPAN)]
        fresh = [state_ref[a, RIM : RIM + BLOCKS_PAD] for a in range(SPAN)]
        for part in (before, after):
            for a in range(SPAN):
                for b in range(SPAN):
                    fresh[a] = fresh[a] + coef[:, slot : slot + 1] * part[b]
                    slot += 1
        for a in range(SPAN):
            state_ref[a, RIM : RIM + BLOCKS_PAD] = fresh[a]
        step *= 2
    last = [state_ref[b, RIM : RIM + BLOCKS_PAD] for b in range(SPAN)]
    for a in range(SPAN):
        total = None
        for b in range(SPAN):
            term = coef[:, slot : slot + 1] * last[b]
            total = term if total is None else total + term
            slot += 1
        flat_ref[a * BLOCKS_PAD : (a + 1) * BLOCKS_PAD] = total
    mixed = jnp.dot(
        mix_ref[0],
        flat_ref[...],
        precision=lax.Precision.HIGHEST,
        preferred_element_type=jnp.float32,
    )
    high = mixed.astype(jnp.bfloat16)
    rest = mixed - high.astype(jnp.float32)
    mid = rest.astype(jnp.bfloat16)
    high_ref[0] = high
    mid_ref[0] = mid
    low_ref[0] = (rest - mid.astype(jnp.float32)).astype(jnp.bfloat16)


def operator_kernel(high_ref, mid_ref, low_ref, early_ref, late_ref, keep_ref, out_ref):
    date = lax.broadcasted_iota(jnp.int32, (high_ref.shape[2], early_ref.shape[1]), 0)
    plus = jnp.where(date == late_ref[...], 1.0, 0.0)
    minus = jnp.where(date == early_ref[...], 1.0, 0.0)
    incidence = (plus - minus).astype(jnp.bfloat16)
    total = jnp.dot(low_ref[0], incidence, preferred_element_type=jnp.float32)
    total += jnp.dot(mid_ref[0], incidence, preferred_element_type=jnp.float32)
    total += jnp.dot(high_ref[0], incidence, preferred_element_type=jnp.float32)
    out_ref[0] = (total * keep_ref[0]).astype(jnp.bfloat16)


def mixing_matrix(gap_dates):
    classes = gap_dates.shape[0]
    dates = jnp.arange(DATES, dtype=jnp.int32)
    gapped = jnp.any(gap_dates[:, :, None] == dates[None, None, :], axis=1)
    earlier = jnp.where(~gapped[:, None, :] & (dates[None, :] < dates[:, None]), dates, -1)
    later = jnp.where(~gapped[:, None, :] & (dates[None, :] > dates[:, None]), dates, DATES)
    left = jnp.max(earlier, axis=2)
    right = jnp.min(later, axis=2)
    ahead = (right - dates).astype(jnp.float32) / corr_length
    behind = (dates - left).astype(jnp.float32) / corr_length
    whole = jnp.sinh(ahead + behind)
    no_left = left < 0
    no_right = right >= DATES
    from_left = jnp.where(no_right, jnp.exp(-behind), jnp.sinh(ahead) / whole)
    from_right = jnp.where(no_left, jnp.exp(-ahead), jnp.sinh(behind) / whole)
    from_left = jnp.where(gapped & ~no_left, from_left, 0.0)
    from_right = jnp.where(gapped & ~no_right, from_right, 0.0)
    place = jnp.arange(SPAN * BLOCKS_PAD, dtype=jnp.int32)
    source = SPAN * (place % BLOCKS_PAD) + place // BLOCKS_PAD
    source = jnp.where(source < DATES, source, -2)
    mix = jnp.where(source == dates[:, None], 1.0, 0.0)[None]
    mix = mix + jnp.where(source == left[:, :, None], from_left[:, :, None], 0.0)
    mix = mix + jnp.where(source == right[:, :, None], from_right[:, :, None], 0.0)
    return jnp.pad(mix, ((0, 0), (0, DATES_PAD - DATES), (0, 0)))


def build_operators(pair_dates, mask_table, gap_dates, own, width):
    classes, pairs = mask_table.shape
    early, late = pair_dates[:, 0], pair_dates[:, 1]
    lost = jnp.any(
        (gap_dates[:, :, None] == early) | (gap_dates[:, :, None] == late), axis=1
    )
    keep = jnp.where(lost, 0.0, mask_table.astype(jnp.float32))
    padded = round_up(pairs, LANES)
    keep_all = jnp.pad(keep, ((0, round_up(classes, 8) - classes), (0, padded - pairs)))
    early_all = jnp.pad(early[None], ((0, 0), (0, padded - pairs)), constant_values=-1)
    late_all = jnp.pad(late[None], ((0, 0), (0, padded - pairs)), constant_values=-1)
    slots = (2 * LEVELS + 1) * SPAN * SPAN
    coef = pl.pallas_call(
        reduction_kernel,
        out_shape=jax.ShapeDtypeStruct((slots, keep_all.shape[0], LANES), jnp.float32),
        compiler_params=pltpu.CompilerParams(vmem_limit_bytes=48 << 20),
    )(keep_all, early_all, late_all)
    coef = jnp.transpose(coef[:, :classes, :BLOCKS_PAD], (1, 2, 0))
    mix = mixing_matrix(gap_dates)
    wide = round_up(DATES, LANES)
    piece = pl.BlockSpec((1, DATES_PAD, LANES), lambda q, j: (q, 0, j))
    shape = jax.ShapeDtypeStruct((classes, DATES_PAD, wide), jnp.bfloat16)
    parts = pl.pallas_call(
        inverse_kernel,
        grid=(classes, wide // LANES),
        in_specs=[
            pl.BlockSpec((1, BLOCKS_PAD, slots), lambda q, j: (q, 0, 0)),
            pl.BlockSpec((1, DATES_PAD, SPAN * BLOCKS_PAD), lambda q, j: (q, 0, 0)),
        ],
        out_specs=[piece] * 3,
        out_shape=[shape] * 3,
        scratch_shapes=[
            pltpu.VMEM((SPAN, BLOCKS_PAD + 2 * RIM, LANES), jnp.float32),
            pltpu.VMEM((SPAN * BLOCKS_PAD, LANES), jnp.float32),
        ],
        compiler_params=pltpu.CompilerParams(vmem_limit_bytes=48 << 20),
    )(coef, mix)
    count = pairs // own[1]
    begin = own[0] * count
    cut = lambda value, fill: jnp.pad(
        lax.dynamic_slice_in_dim(value, begin, count, 1),
        ((0, 0), (0, width - count)),
        constant_values=fill,
    )
    full = pl.BlockSpec((1, DATES_PAD, wide), lambda q: (q, 0, 0))
    line = pl.BlockSpec((1, width), lambda q: (0, 0))
    return pl.pallas_call(
        operator_kernel,
        grid=(classes,),
        in_specs=[full] * 3 + [line] * 2 + [pl.BlockSpec((1, 1, width), lambda q: (q, 0, 0))],
        out_specs=pl.BlockSpec((1, DATES_PAD, width), lambda q: (q, 0, 0)),
        out_shape=jax.ShapeDtypeStruct((classes, DATES_PAD, width), jnp.bfloat16),
        compiler_params=pltpu.CompilerParams(vmem_limit_bytes=48 << 20),
    )(*parts, cut(early[None], -1), cut(late[None], -1), cut(keep, 0.0)[:, None, :])


def edge_rows(value, axis, width, order=None):
    count, length = lax.axis_size(axis), value.shape[0] if order is None else value.shape[2]
    dim = 0 if order is None else 2
    up = [(i, (i + 1) % count) for i in range(count - 1)]
    down = [(j, i) for i, j in up]
    last = lax.slice_in_dim(value, length - width, length, axis=dim)
    leading = lax.slice_in_dim(value, 0, width, axis=dim)
    if order is not None:
        last, leading = jnp.transpose(last, order), jnp.transpose(leading, order)
    return lax.ppermute(last, axis, up), lax.ppermute(leading, axis, down)


def looks_kernel(pairs, planes_ref, top_ref, bottom_ref, band_ref, out_ref, box_ref):
    batch, strip, columns = planes_ref.shape[1:]
    band = band_ref[...]
    halves = columns // LANES
    rim = top_ref.shape[1]
    edges = []
    for c in range(2):
        along = jnp.dot(
            planes_ref[c].reshape(batch * strip, columns),
            band,
            preferred_element_type=jnp.float32,
        )
        for h in range(halves):
            box_ref[c, h] = along[:, h * LANES : (h + 1) * LANES]
        edges.append(
            [
                [jnp.dot(ref[c, i], band, preferred_element_type=jnp.float32) for i in range(rim)]
                for ref in (top_ref, bottom_ref)
            ]
        )
    spot = lax.broadcasted_iota(jnp.int32, (batch, LANES), 0) + pl.program_id(0) * batch
    valid = spot < pairs
    for h in range(halves):
        lanes = slice(h * LANES, (h + 1) * LANES)

        def row(c, r):
            if r < 0:
                return edges[c][0][r + rim][:, lanes]
            if r >= strip:
                return edges[c][1][r - strip][:, lanes]
            return box_ref[c, h, pl.ds(r, batch, stride=strip), :]

        lines = [[row(c, r) for r in range(-rim, -rim + 4)] for c in range(2)]
        for r in range(strip):
            boxed = []
            for c in range(2):
                lines[c].append(row(c, r + rim))
                a, b, d, e, f = lines[c]
                boxed.append((a + b) + (d + e) + f)
                lines[c].pop(0)
            power = boxed[0] * boxed[0] + boxed[1] * boxed[1]
            looks = boxed[1] * lax.rsqrt(jnp.maximum(power, 1.0))
            out_ref[r, :, lanes] = jnp.where(valid, looks, 0.0).astype(jnp.bfloat16)


def multilook(interferograms, top, bottom, width):
    pairs, strip, columns = interferograms.shape[1:]
    batch = width // (width // LANES + 2) if width % (width // LANES + 2) == 0 else LANES
    batch = batch if batch % 16 == 0 else LANES
    rim = top.shape[1]
    spots = np.arange(columns)
    band = (np.abs(spots[:, None] - spots[None, :]) <= 2).astype(ml_dtypes.bfloat16)
    edge = pl.BlockSpec((2, rim, batch, columns), lambda j: (0, 0, j, 0))
    return pl.pallas_call(
        functools.partial(looks_kernel, pairs),
        grid=(width // batch,),
        in_specs=[
            pl.BlockSpec((2, batch, strip, columns), lambda j: (0, j, 0, 0)),
            edge,
            edge,
            pl.BlockSpec((columns, columns), lambda j: (0, 0)),
        ],
        out_specs=pl.BlockSpec((strip, batch, columns), lambda j: (0, j, 0)),
        out_shape=jax.ShapeDtypeStruct((strip, width, columns), jnp.bfloat16),
        scratch_shapes=[
            pltpu.VMEM((2, columns // LANES, batch * strip, LANES), jnp.float32)
        ],
        compiler_params=pltpu.CompilerParams(vmem_limit_bytes=48 << 20),
    )(interferograms, top, bottom, jnp.asarray(band))


def series_kernel(half_ref, operator_ref, looks_ref, class_ref, out_ref):
    total = jnp.zeros((operator_ref.shape[1], looks_ref.shape[2]), jnp.float32)
    for q in range(operator_ref.shape[0]):
        solved = jnp.dot(operator_ref[q], looks_ref[0], preferred_element_type=jnp.float32)
        total = jnp.where(class_ref[0] == q, solved, total)
    out_ref[0] = total[: out_ref.shape[1]]


def invert(operators, looks, pattern_ids, half, rows):
    classes, dates, width = operators.shape
    columns = looks.shape[2]
    return pl.pallas_call(
        series_kernel,
        grid_spec=pltpu.PrefetchScalarGridSpec(
            num_scalar_prefetch=1,
            grid=(rows,),
            in_specs=[
                pl.BlockSpec((classes, dates, width), lambda r, h: (0, 0, 0)),
                pl.BlockSpec((1, width, columns), lambda r, h: (h[0] * rows + r, 0, 0)),
                pl.BlockSpec((1, 1, columns), lambda r, h: (h[0] * rows + r, 0, 0)),
            ],
            out_specs=pl.BlockSpec((1, DATES, columns), lambda r, h: (r, 0, 0)),
        ),
        out_shape=jax.ShapeDtypeStruct((rows, DATES, columns), jnp.float32),
        compiler_params=pltpu.CompilerParams(vmem_limit_bytes=48 << 20),
        cost_estimate=pl.CostEstimate(
            flops=2 * classes * dates * width * columns * rows,
            bytes_accessed=2 * rows * width * columns + 4 * rows * dates * columns,
            transcendentals=0,
        ),
    )(jnp.reshape(half, (1,)), operators, looks, pattern_ids[:, None, :])


def gauss_taps():
    spots = np.arange(-RADIUS, RADIUS + 1)
    raw = np.exp(-spots * spots / (2.0 * gauss_width * gauss_width))
    return raw / raw.sum()


def screen_kernel(taps, series_ref, before_ref, after_ref, high_ref, low_ref, out_ref):
    rows, tile, columns = series_ref.shape
    lines = [before_ref[i].astype(jnp.float32) for i in range(RADIUS)]
    lines += [series_ref[i] for i in range(rows)]
    lines += [after_ref[i].astype(jnp.float32) for i in range(RADIUS)]
    for r in range(rows):
        total = taps[RADIUS] * lines[r + RADIUS]
        for a in range(RADIUS):
            total += taps[a] * (lines[r + a] + lines[r + 2 * RADIUS - a])
        high = total.astype(jnp.bfloat16)
        low = (total - high.astype(jnp.float32)).astype(jnp.bfloat16)
        screen = jnp.dot(low, high_ref[...], preferred_element_type=jnp.float32)
        screen += jnp.dot(high, low_ref[...], preferred_element_type=jnp.float32)
        screen += jnp.dot(high, high_ref[...], preferred_element_type=jnp.float32)
        out_ref[r] = series_ref[r] - screen


def remove_screen(series, before, after):
    rows, dates, columns = series.shape
    taps = gauss_taps()
    spots = np.arange(columns)
    lag = spots[:, None] - spots[None, :]
    band = np.where(np.abs(lag) <= RADIUS, taps[np.clip(lag, -RADIUS, RADIUS) + RADIUS], 0.0)
    band = band.astype(np.float32)
    high = band.astype(ml_dtypes.bfloat16)
    low = (band - high.astype(np.float32)).astype(ml_dtypes.bfloat16)
    tile = 64
    piece = lambda count: pl.BlockSpec((count, tile, columns), lambda t: (0, t, 0))
    square = pl.BlockSpec((columns, columns), lambda t: (0, 0))
    return pl.pallas_call(
        functools.partial(screen_kernel, [float(x) for x in taps]),
        grid=(-(-dates // tile),),
        in_specs=[piece(rows), piece(RADIUS), piece(RADIUS), square, square],
        out_specs=piece(rows),
        out_shape=jax.ShapeDtypeStruct(series.shape, jnp.float32),
        compiler_params=pltpu.CompilerParams(vmem_limit_bytes=48 << 20),
    )(series, before, after, jnp.asarray(high), jnp.asarray(low))


def body(interferograms, pair_dates, mask_table, gap_dates, pattern_ids):
    pairs, strip = interferograms.shape[1:3]
    shares = lax.axis_size("pairs")
    place = lax.axis_index("pairs")
    my_rows = strip // shares
    width = round_up(pairs, LANES)
    top, bottom = edge_rows(interferograms, "rows", 2, (0, 2, 1, 3))
    operators = build_operators(pair_dates, mask_table, gap_dates, (place, shares), width)
    looks = multilook(interferograms, top, bottom, width)
    series = None
    for turn in range(shares - 1, -1, -1):
        half = (place + turn) % shares
        part = invert(operators, looks, pattern_ids, half, my_rows)
        if turn:
            part = lax.ppermute(part, "pairs", [(i, (i + turn) % shares) for i in range(shares)])
        series = part if series is None else series + part
    before, after = edge_rows_bf16(series)
    return remove_screen(series, before, after)


def edge_rows_bf16(series):
    return edge_rows(series.astype(jnp.bfloat16), ("rows", "pairs"), RADIUS)


def solution(mesh):
    placed = (
        P(None, "pairs", ("blocks", "rows"), None),
        P(),
        P(),
        P(),
        P(("blocks", "rows"), None),
    )
    return jax.shard_map(
        body,
        mesh=mesh,
        in_specs=placed,
        out_specs=P(("blocks", "rows", "pairs"), None, None),
        check_vma=False,
    )
```

time: 784 us -> 165 us (0.21); the launches traced: 774 us -> 164 us
  other arithmetic: 490 us -> 15.7 us
  local copies, waits for them, and re-layouts: 121 us -> 22.9 us
  matrix products: 93.3 us -> 0 us
  Pallas kernels: 0 us -> 92.9 us
  loops' own time: 16.6 us -> 0 us
  between operations: 13.8 us -> 0.34 us
  blocking collectives: 9.55 us -> 0 us
    another operation x60 -> x0, other arithmetic: 321 us -> none  [the longest x20 101 us: single(): factor_two = jnp.linalg.cholesky(masked)]
    add x5 -> x1, other arithmetic: 119 us -> 0.71 us  [mixing_matrix(): mix + jnp.where(source == right[:, :, None], from_right[:, :, None], 0.0)]
    pallas_call x0 -> x7, Pallas kernels: none -> 92.9 us  [the longest x1 49.7 us: build_operators(): pl.pallas_call(inverse_kernel, grid=(classes, wide // LANES), in_specs=[p...]
    dynamic_update_slice x4 -> x0, local copies, waits for them, and re-layouts: 58.5 us -> none  [build_operators(): return lax.map(single, (mask_rows, gapped)).astype(jnp.bfloat16)]
    another operation x56 -> x0, matrix products: 50.8 us -> none  [the longest x20 28 us: single(): solved = jax.scipy.linalg.cho_solve((factor, True), weighted.T)]
    dot_general x9 -> x0, matrix products: 42.5 us -> none  [the longest x1 11.5 us: body(): jnp.einsum('qtk,krc->rqtc', operators, lax.all_to_all(looks, 'pairs', spl...]
    convert_element_type x7 -> x1, other arithmetic: 29.2 us -> 4.11 us  [edge_rows_bf16(): return edge_rows(series.astype(jnp.bfloat16), ('rows', 'pairs'), RADIUS)]
    another operation x52 -> x0, local copies, waits for them, and re-layouts: 20.4 us -> none
  transfers between devices with their start and end apart: 5 -> 5, of which waited for: 2 -> 1; matrix products, arithmetic and copies ran while one was open for 84% -> 9% of each run, Pallas kernels for 0% -> 39%
where the time goes in v1:
time: 165 us; the launch traced here: 164 us
  Pallas kernels  92.9 us (56%)
  local copies, waits for them, and re-layouts  22.9 us (14%)
  waiting for transfers between devices  18.6 us (11%)
  other arithmetic  15.7 us (10%)
  starting transfers between devices  13.4 us (8%)
    pallas_call x1, Pallas kernels, build_operators(): pl.pallas_call(inverse_kernel, grid=(classes, wide // LANES), in_specs=[p...  49.7 us
    ppermute x4, waiting for transfers between devices, edge_rows(): return (lax.ppermute(last, axis, up), lax.ppermute(leading, axis, down))  18.6 us
    pallas_call x1, Pallas kernels, multilook(): pl.pallas_call(functools.partial(looks_kernel, pairs), grid=(width // bat...  17.1 us
    pallas_call x2, Pallas kernels, invert(): pl.pallas_call(series_kernel, grid_spec=pltpu.PrefetchScalarGridSpec(num_...  14.7 us
    ppermute x4, starting transfers between devices, edge_rows(): return (lax.ppermute(last, axis, up), lax.ppermute(leading, axis, down))  12.5 us
    reduce_min x1, other arithmetic, mixing_matrix(): right = jnp.min(later, axis=2)  10.2 us
    transpose x1, local copies, waits for them, and re-layouts, edge_rows(): last, leading = (jnp.transpose(last, order), jnp.transpose(leading, order))  7.92 us
    pallas_call x1, Pallas kernels, remove_screen(): pl.pallas_call(functools.partial(screen_kernel, [float(x) for x in taps])...  5.37 us
  transfers between devices with their start and end apart: 5, of which 1 were waited for; matrix products, arithmetic and copies ran while one was open for 9% of the time, Pallas kernels for 39%

profile of v1, /device:TPU:1, one launch (start us, length us, event | category | flops | bytes accessed | tf_op | source)
XLA Modules:
  0.0 163.9 jit_solution(10012487951500069160)
XLA Ops:
  0.0 7.9 %slice_bitcast_fusion = (bf16[2,2,750,256]{3,1,2,0:T(2,128)(2,1)}, bf16[2,2,750,256]{3,1,2,0:T(2,128)(2,1)}) fusion(bf16[2,750,16,256]{3,2,1,0:T(8,128)(2,1)} %planes_ref.1), kind=kLoop, calls=%fused_computation.4 | loop fusion | bytes 6144000 | tf_op jit(solution)/shard_map/transpose | solution.py:271
  7.9 5.1 %collective-permute-start = (bf16[2,2,750,256]{3,1,2,0:T(2,128)(2,1)}, bf16[2,2,750,256]{3,1,2,0:T(2,128)(2,1)}, u32[]{:S(2)}, u32[]{:S(2)}) collective-permute-start(bf16[2,2,750,256]{3,1,2,0:T(2,128)(2,1)} %get-tuple-element.18), channel_id=1, source_target_pairs={{0,2},{2,4},{4,6},{6,8},{8,10},{10,12},{12,14},{1,3},{3,5},{5,7},{... | collective-permute-start | bytes 4608008 | tf_op jit(solution)/shard_map/ppermute | solution.py:272
  13.0 1.3 collective-permute-start.1
  14.3 0.1 iota_compare_fusion
  14.4 0.1 copy.19
  14.5 0.1 fusion.1
  14.7 10.2 %select_reduce_fusion = (s32[4,300]{0,1:T(8,128)S(1)}, s32[4,300]{0,1:T(8,128)S(1)}) fusion(pred[300,300]{1,0:T(8,128)(4,1)S(1)} %get-tuple-element.31, pred[4,300]{1,0:T(4,128)(4,1)S(1)} %not.23, pred[300,300]{1,0:T(8,128)(4,1)S(1)} %get-tuple-element.32), kind=kLoop, calls=%fused_computation.2 | loop fusion | flops 2157600 | bytes 190800 | tf_op jit(solution)/shard_map/reduce_min | solution.py:188
  24.9 0.1 copy.22
  25.0 0.1 copy.24
  25.1 0.1 fusion
  25.1 0.1 select_select_fusion.1
  25.2 0.7 select_add_fusion
  25.9 0.0 copy-start.9
  25.9 0.0 copy-start.7
  25.9 0.1 pad.29.mix_ref
  26.1 0.6 copy-done.9
  26.7 0.3 or_reduce_fusion
  27.1 0.0 copy-start.8
  27.1 2.2 %shard_map.82 = f32[325,8,128]{2,1,0:T(8,128)S(1)} custom-call(f32[8,1536]{1,0:T(8,128)S(1)} %pad.26.keep_ref, s32[1,1536]{1,0:T(1,128)S(1)} %pad.27.early_ref, s32[1,1536]{1,0:T(1,128)S(1)} %pad.28.late_ref), custom_call_target="tpu_custom_call" | custom-call | tf_op jit(solution)/shard_map/pallas_call | solution.py:219
  29.3 0.1 slice.28
  29.4 0.3 copy.33
  29.7 0.1 constant_dynamic-slice_fusion
  29.8 0.1 dynamic-slice_bitcast_fusion
  30.0 49.7 %shard_map.83 = (bf16[4,304,384]{2,1,0:T(8,128)(2,1)S(1)}, bf16[4,304,384]{2,1,0:T(8,128)(2,1)S(1)}, bf16[4,304,384]{2,1,0:T(8,128)(2,1)S(1)}) custom-call(f32[4,64,325]{2,1,0:T(8,128)S(1)} %bitcast.15, f32[4,304,320]{2,1,0:T(8,128)S(1)} %pad.29.mix_ref), custom_call_target="tpu_custom_call" | custom-call | tf_op jit(solution)/shard_map/pallas_call | solution.py:229
  79.7 0.9 copy-done
  80.6 0.9 copy-done.2
  81.5 1.2 copy-done.1
  82.7 1.2 copy-done.3
  83.9 3.9 %shard_map.84.operator_ref = bf16[4,304,768]{2,1,0:T(8,128)(2,1)S(1)} custom-call(bf16[4,304,384]{2,1,0:T(8,128)(2,1)S(1)} %get-tuple-element.8.high_ref, bf16[4,304,384]{2,1,0:T(8,128)(2,1)S(1)} %copy-done.1, bf16[4,304,384]{2,1,0:T(8,128)(2,1)S(1)} %copy-done.3, s32[1,768]{1,0:T(1,128)S(1)} %pad.30.early_ref, s32[1,768]{1,0:T(1,128)S(1)} %pad.31.late_ref, ...), custom_call_target="tpu_custom_call" | custom-call | tf_op jit(solution)/shard_map/pallas_call | solution.py:253
  87.8 0.0 collective-permute-done
  87.8 1.6 copy.28.top_ref
  89.4 0.0 copy-start.6
  89.4 0.0 collective-permute-done.1
  89.4 1.6 %copy.29.bottom_ref = bf16[2,2,750,256]{3,2,1,0:T(8,128)(2,1)S(1)} copy(bf16[2,2,750,256]{3,1,2,0:T(2,128)(2,1)} %collective-permute-done.1) | data formatting | bytes 3072000 | tf_op jit(solution)/shard_map/ppermute | solution.py:272
  91.1 17.1 %shard_map.85.looks_ref = bf16[16,768,256]{2,1,0:T(8,128)(2,1)} custom-call(bf16[2,750,16,256]{3,2,1,0:T(8,128)(2,1)} %planes_ref.1, bf16[2,2,750,256]{3,2,1,0:T(8,128)(2,1)S(1)} %copy.28.top_ref, bf16[2,2,750,256]{3,2,1,0:T(8,128)(2,1)S(1)} %copy.29.bottom_ref, bf16[256,256]{1,0:T(8,128)(2,1)S(1)} %copy-done.6), custom_call_target="tpu_custom_call" | custom-call | tf_op jit(solution)/shard_map/pallas_call | solution.py:328
  108.1 7.4 %shard_map.86 = f32[8,300,256]{2,1,0:T(8,128)S(1)} custom-call(s32[1]{0:T(128)} %bitcast.half_ref, bf16[4,304,768]{2,1,0:T(8,128)(2,1)S(1)} %shard_map.84.operator_ref, bf16[16,768,256]{2,1,0:T(8,128)(2,1)} %shard_map.85.looks_ref, s32[16,1,256]{2,1,0:T(1,128)S(1)} %broadcast_in_dim.96.class_ref), custom_call_target="tpu_custom_call" | custom-call | flops 3825205248 | bytes 5636096 | tf_op jit(solution)/shard_map/pallas_call | solution.py:357
  115.5 2.9 %copy.30 = f32[8,300,256]{2,0,1:T(8,128)} copy(f32[8,300,256]{2,1,0:T(8,128)S(1)} %shard_map.86) | data formatting | bytes 4915200 | tf_op jit(solution)/shard_map/pallas_call | solution.py:357
  118.4 1.0 collective-permute-start.2
  119.3 7.4 %shard_map.87 = f32[8,300,256]{2,1,0:T(8,128)S(1)} custom-call(s32[1]{0:T(128)} %bitcast.8.half_ref, bf16[4,304,768]{2,1,0:T(8,128)(2,1)S(1)} %shard_map.84.operator_ref, bf16[16,768,256]{2,1,0:T(8,128)(2,1)} %shard_map.85.looks_ref, s32[16,1,256]{2,1,0:T(1,128)S(1)} %broadcast_in_dim.96.class_ref), custom_call_target="tpu_custom_call" | custom-call | flops 3825205248 | bytes 5636096 | tf_op jit(solution)/shard_map/pallas_call | solution.py:357
  126.7 0.0 collective-permute-done.2
  126.7 4.1 %fusion.17 = (bf16[8,300,256]{2,1,0:T(8,128)(2,1)S(1)}, f32[8,300,256]{2,1,0:T(8,128)}) fusion(f32[8,300,256]{2,1,0:T(8,128)S(1)} %shard_map.87, f32[8,300,256]{2,0,1:T(8,128)} %collective-permute-done.2), kind=kLoop, calls=%fused_computation.53 | loop fusion | flops 1228800 | bytes 8601600 | tf_op jit(solution)/shard_map/convert_element_type | solution.py:445
  130.8 0.1 fusion.18
  131.0 4.2 %collective-permute-start.3 = (bf16[6,300,256]{2,1,0:T(8,128)(2,1)S(1)}, bf16[6,300,256]{2,1,0:T(8,128)(2,1)S(1)}, u32[]{:S(2)}, u32[]{:S(2)}) collective-permute-start(bf16[6,300,256]{2,1,0:T(8,128)(2,1)S(1)} %get-tuple-element.20), channel_id=1, source_target_pairs={{0,1},{1,2},{2,3},{3,4},{4,5},{5,6},{6,7},{7,8},{8,9},{9,10},{10,1... | collective-permute-start | bytes 2764808 | tf_op jit(solution)/shard_map/ppermute | solution.py:272
  135.1 1.9 %collective-permute-start.4 = (bf16[6,300,256]{2,1,0:T(8,128)(2,1)S(1)}, bf16[6,300,256]{2,1,0:T(8,128)(2,1)S(1)}, u32[]{:S(2)}, u32[]{:S(2)}) collective-permute-start(bf16[6,300,256]{2,1,0:T(8,128)(2,1)S(1)} %get-tuple-element.19), channel_id=1, source_target_pairs={{1,0},{2,1},{3,2},{4,3},{5,4},{6,5},{7,6},{8,7},{9,8},{10,9},{11,1... | collective-permute-start | bytes 2764808 | tf_op jit(solution)/shard_map/ppermute | solution.py:272
  137.0 18.6 %collective-permute-done.3.before_ref = bf16[6,300,256]{2,1,0:T(8,128)(2,1)S(1)} collective-permute-done((bf16[6,300,256]{2,1,0:T(8,128)(2,1)S(1)}, bf16[6,300,256]{2,1,0:T(8,128)(2,1)S(1)}, u32[]{:S(2)}, u32[]{:S(2)}) %collective-permute-start.3) | collective-permute-done | bytes 921632 | tf_op jit(solution)/shard_map/ppermute | solution.py:272
  155.6 0.0 collective-permute-done.4.after_ref
  155.6 5.4 %shard_map.88 = f32[8,300,256]{2,1,0:T(8,128)S(1)} custom-call(f32[8,300,256]{2,1,0:T(8,128)} %get-tuple-element.16.series_ref, bf16[6,300,256]{2,1,0:T(8,128)(2,1)S(1)} %collective-permute-done.3.before_ref, bf16[6,300,256]{2,1,0:T(8,128)(2,1)S(1)} %collective-permute-done.4.after_ref, bf16[256,256]{1,0:T(8,128)(2,1)S(1)} %copy-done.4, ...), custom_call_target="tpu_custom_call" | custom-call | tf_op jit(solution)/shard_map/pallas_call | solution.py:414
  161.0 2.9 %copy.32 = f32[8,300,256]{2,0,1:T(8,128)} copy(f32[8,300,256]{2,1,0:T(8,128)S(1)} %shard_map.88) | data formatting | bytes 4915200 | tf_op jit(solution)/shard_map/pallas_call | solution.py:414
  (25 shorter events, 0.2 us)
Async XLA Ops:
  0.0 14.4 %copy-start.10 = (s32[4,30]{1,0:T(4,128)S(1)}, s32[4,30]{1,0:T(4,128)}, u32[]{:S(2)}) copy-start(s32[4,30]{1,0:T(4,128)} %param.11) | copy-start | bytes 1444
  7.9 79.9 %collective-permute-start = (bf16[2,2,750,256]{3,1,2,0:T(2,128)(2,1)}, bf16[2,2,750,256]{3,1,2,0:T(2,128)(2,1)}, u32[]{:S(2)}, u32[]{:S(2)}) collective-permute-start(bf16[2,2,750,256]{3,1,2,0:T(2,128)(2,1)} %get-tuple-element.18), channel_id=1, source_target_pairs={{0,2},{2,4},{4,6},{6,8},{8,10},{10,12},{12,14},{1,3},{3,5},{5,7},{... | collective-permute-start | bytes 4608008 | tf_op jit(solution)/shard_map/ppermute | solution.py:272
  13.0 76.4 %collective-permute-start.1 = (bf16[2,2,750,256]{3,1,2,0:T(2,128)(2,1)}, bf16[2,2,750,256]{3,1,2,0:T(2,128)(2,1)}, u32[]{:S(2)}, u32[]{:S(2)}) collective-permute-start(bf16[2,2,750,256]{3,1,2,0:T(2,128)(2,1)} %get-tuple-element.17), channel_id=1, source_target_pairs={{2,0},{4,2},{6,4},{8,6},{10,8},{12,10},{14,12},{3,1},{5,3},{7,5},{... | collective-permute-start | bytes 4608008 | tf_op jit(solution)/shard_map/ppermute | solution.py:272
  25.9 0.7 copy-start.9
  25.9 1.1 copy-start.7
  27.1 2.8 %copy-start.8 = (s32[16,256]{1,0:T(8,128)S(1)}, s32[16,256]{1,0:T(8,128)}, u32[]{:S(2)}) copy-start(s32[16,256]{1,0:T(8,128)} %param.12) | copy-start | bytes 49156
  79.6 1.0 copy-start
  80.6 0.9 copy-start.2
  81.5 1.2 copy-start.1
  82.7 1.2 copy-start.3
  89.4 1.7 %copy-start.6 = (bf16[256,256]{1,0:T(8,128)(2,1)S(1)}, bf16[256,256]{1,0:T(8,128)(2,1)}, u32[]{:S(2)}) copy-start(bf16[256,256]{1,0:T(8,128)(2,1)} %constant.99.clone.band_ref) | copy-start | bytes 393220
  118.4 8.3 %collective-permute-start.2 = (f32[8,300,256]{2,0,1:T(8,128)}, f32[8,300,256]{2,0,1:T(8,128)}, u32[]{:S(2)}, u32[]{:S(2)}) collective-permute-start(f32[8,300,256]{2,0,1:T(8,128)} %copy.30), channel_id=1, source_target_pairs={{0,1},{1,0},{2,3},{3,2},{4,5},{5,4},{6,7},{7,6},{8,9},{9,8},{10,11... | collective-permute-start | bytes 7372808 | tf_op jit(solution)/shard_map/ppermute | solution.py:438
  130.8 24.8 %copy-start.4 = (bf16[256,256]{1,0:T(8,128)(2,1)S(1)}, bf16[256,256]{1,0:T(8,128)(2,1)}, u32[]{:S(2)}) copy-start(bf16[256,256]{1,0:T(8,128)(2,1)} %constant.100.clone.high_ref) | copy-start | bytes 393220
  130.8 24.8 %copy-start.5 = (bf16[256,256]{1,0:T(8,128)(2,1)S(1)}, bf16[256,256]{1,0:T(8,128)(2,1)}, u32[]{:S(2)}) copy-start(bf16[256,256]{1,0:T(8,128)(2,1)} %constant.101.clone.low_ref) | copy-start | bytes 393220
  131.0 24.7 %collective-permute-start.3 = (bf16[6,300,256]{2,1,0:T(8,128)(2,1)S(1)}, bf16[6,300,256]{2,1,0:T(8,128)(2,1)S(1)}, u32[]{:S(2)}, u32[]{:S(2)}) collective-permute-start(bf16[6,300,256]{2,1,0:T(8,128)(2,1)S(1)} %get-tuple-element.20), channel_id=1, source_target_pairs={{0,1},{1,2},{2,3},{3,4},{4,5},{5,6},{6,7},{7,8},{8,9},{9,10},{10,1... | collective-permute-start | bytes 2764808 | tf_op jit(solution)/shard_map/ppermute | solution.py:272
  135.1 20.5 %collective-permute-start.4 = (bf16[6,300,256]{2,1,0:T(8,128)(2,1)S(1)}, bf16[6,300,256]{2,1,0:T(8,128)(2,1)S(1)}, u32[]{:S(2)}, u32[]{:S(2)}) collective-permute-start(bf16[6,300,256]{2,1,0:T(8,128)(2,1)S(1)} %get-tuple-element.19), channel_id=1, source_target_pairs={{1,0},{2,1},{3,2},{4,3},{5,4},{6,5},{7,6},{8,7},{9,8},{10,9},{11,1... | collective-permute-start | bytes 2764808 | tf_op jit(solution)/shard_map/ppermute | solution.py:272

commit v2 on v1

v2 whole, which is shorter than its diff:
```python
import functools

import jax
import ml_dtypes
import numpy as np
import jax.numpy as jnp
from jax import lax
from jax.experimental import pallas as pl
from jax.experimental.pallas import tpu as pltpu
from jax.sharding import PartitionSpec as P

DATES = 300
NPAT = 4
SPAN = 5
RADIUS = 6
LANES = 128
BLOCKS = DATES // SPAN
BLOCKS_PAD = 64
DATES_PAD = 304
LEVELS = 6
RIM = 32
SUB = 8
WIDE = 384


damping = 0.5
corr_length = 10.0
gauss_width = 2.0


def round_up(value, unit):
    return -(-value // unit) * unit


def block_matmul(left, right, transposed=False):
    size = len(left)
    out = []
    for a in range(size):
        row = []
        for b in range(size):
            total = None
            for m in range(size):
                term = left[a][m] * (right[b][m] if transposed else right[m][b])
                total = term if total is None else total + term
            row.append(total)
        out.append(row)
    return out


def block_inverse(matrix):
    size = len(matrix)
    work = [list(row) for row in matrix]
    for k in range(size):
        pivot = 1.0 / work[k][k]
        work[k] = [pivot if j == k else work[k][j] * pivot for j in range(size)]
        for i in range(size):
            if i != k:
                factor = work[i][k]
                work[i] = [
                    -factor * pivot if j == k else work[i][j] - factor * work[k][j]
                    for j in range(size)
                ]
    return work


def moved(blocks, shift):
    return [[pltpu.roll(item, shift % LANES, 1) for item in row] for row in blocks]


def nearest_weights(gap_ref, near_ref):
    gaps = gap_ref[...]
    shape = near_ref.shape[1:]
    dates = lax.broadcasted_iota(jnp.int32, shape, 1)
    gapped = jnp.zeros(shape, jnp.float32)
    for g in range(gaps.shape[1]):
        gapped = jnp.where(gaps[:, g : g + 1] == dates, 1.0, gapped)
    seen = (gapped < 0.5) & (dates < DATES)
    day = dates.astype(jnp.float32)
    left = jnp.where(seen, day, -1.0)
    right = jnp.where(seen, day, float(DATES))
    step = 1
    while step <= gaps.shape[1]:
        left = jnp.maximum(left, jnp.where(dates >= step, pltpu.roll(left, step, 1), -1.0))
        right = jnp.minimum(
            right,
            jnp.where(
                dates < shape[1] - step, pltpu.roll(right, shape[1] - step, 1), float(DATES)
            ),
        )
        step *= 2
    ahead = (right - day) / corr_length
    behind = (day - left) / corr_length
    sinh = lambda x: 0.5 * (jnp.exp(x) - jnp.exp(-x))
    whole = sinh(jnp.maximum(ahead + behind, 1.0 / corr_length))
    no_left = left < 0.0
    no_right = right >= float(DATES)
    from_left = jnp.where(no_right, jnp.exp(-behind), sinh(ahead) / whole)
    from_right = jnp.where(no_left, jnp.exp(-ahead), sinh(behind) / whole)
    near_ref[0] = left
    near_ref[1] = right
    near_ref[2] = jnp.where((gapped > 0.5) & ~no_left, from_left, 0.0)
    near_ref[3] = jnp.where((gapped > 0.5) & ~no_right, from_right, 0.0)


def reduction_kernel(keep_ref, early_ref, late_ref, gap_ref, coef_ref, near_ref):
    nearest_weights(gap_ref, near_ref)
    early = early_ref[...]
    span = late_ref[...] - early
    keep = keep_ref[...]
    classes = keep.shape[0]
    picked = jnp.concatenate(
        [jnp.where(span == d, keep, 0.0) for d in range(1, SPAN + 1)], axis=0
    ).astype(jnp.bfloat16)
    count = {}
    for a in range(SPAN):
        date = SPAN * lax.broadcasted_iota(jnp.int32, (LANES, early.shape[1]), 0) + a
        hot = jnp.where(date == early, 1.0, 0.0).astype(jnp.bfloat16)
        counts = lax.dot_general(
            picked, hot, (((1,), (1,)), ((), ())), preferred_element_type=jnp.float32
        )
        for d in range(1, SPAN + 1):
            count[d, a] = counts[(d - 1) * classes : d * classes]
    diagonal, upper = [], []
    for a in range(SPAN):
        total = damping
        for d in range(1, SPAN + 1):
            total = total + count[d, a]
            if a >= d:
                total = total + count[d, a - d]
            else:
                total = total + pltpu.roll(count[d, a - d + SPAN], 1, 1)
        diagonal.append(
            [total if b == a else -count[abs(b - a), min(a, b)] for b in range(SPAN)]
        )
        zero = jnp.zeros_like(total)
        upper.append([-count[SPAN + b - a, a] if b <= a else zero for b in range(SPAN)])
    slot = 0
    step = 1
    while step < BLOCKS:
        inverse = block_inverse(diagonal)
        flipped = [list(row) for row in zip(*upper)]
        below = block_matmul(flipped, inverse)
        gamma = [[-x for x in row] for row in block_matmul(upper, moved(inverse, -step))]
        alpha = [[-x for x in row] for row in moved(below, step)]
        first = moved(block_matmul(below, upper), step)
        second = block_matmul(gamma, upper, transposed=True)
        diagonal = [
            [diagonal[a][b] - first[a][b] + second[a][b] for b in range(SPAN)]
            for a in range(SPAN)
        ]
        upper = block_matmul(gamma, moved(upper, -step))
        for part in (alpha, gamma):
            for row in part:
                for item in row:
                    coef_ref[slot] = item
                    slot += 1
        step *= 2
    for row in block_inverse(diagonal):
        for item in row:
            coef_ref[slot] = item
            slot += 1


def reaching(step, first):
    low = SPAN * (first - (step - 1))
    high = SPAN * (first + SUB + step - 1)
    return [t for t in range(WIDE // LANES) if high > t * LANES and low < (t + 1) * LANES]


def inverse_kernel(coef_ref, mix_ref, early_ref, late_ref, keep_ref, out_ref, state_ref, flat_ref):
    state_ref[...] = jnp.zeros_like(state_ref)
    column = lax.broadcasted_iota(jnp.int32, (BLOCKS_PAD, WIDE), 1)
    date = SPAN * lax.broadcasted_iota(jnp.int32, (BLOCKS_PAD, WIDE), 0)
    for a in range(SPAN):
        state_ref[0, a, RIM : RIM + BLOCKS_PAD] = jnp.where(date + a == column, 1.0, 0.0)
    slot = 0
    step = 1
    turn = 0
    square = SPAN * SPAN
    while step < BLOCKS:
        for first in range(0, BLOCKS_PAD, SUB):
            rows = slice(RIM + first, RIM + first + SUB)
            coef = coef_ref[0, first : first + SUB]
            sides = []
            if first + SUB > step:
                sides.append((slot, -step))
            if first + step < BLOCKS:
                sides.append((slot + square, step))
            tiles = [slice(t * LANES, (t + 1) * LANES) for t in reaching(2 * step, first)]
            fresh = [[state_ref[turn, a, rows, lanes] for lanes in tiles] for a in range(SPAN)]
            for base, shift in sides:
                near = slice(RIM + first + shift, RIM + first + shift + SUB)
                for b in range(SPAN):
                    other = [state_ref[turn, b, near, lanes] for lanes in tiles]
                    for a in range(SPAN):
                        at = base + a * SPAN + b
                        factor = jnp.broadcast_to(coef[:, at : at + 1], (SUB, LANES))
                        fresh[a] = [x + factor * y for x, y in zip(fresh[a], other)]
            for a in range(SPAN):
                for lanes, value in zip(tiles, fresh[a]):
                    state_ref[1 - turn, a, rows, lanes] = value
        slot += 2 * square
        step *= 2
        turn = 1 - turn
    for first in range(0, BLOCKS_PAD, SUB):
        coef = coef_ref[0, first : first + SUB]
        rows = slice(RIM + first, RIM + first + SUB)
        last = [state_ref[turn, b, rows] for b in range(SPAN)]
        for a in range(SPAN):
            total = None
            for b in range(SPAN):
                at = slot + a * SPAN + b
                term = coef[:, at : at + 1] * last[b]
                total = term if total is None else total + term
            flat_ref[a * BLOCKS_PAD + first : a * BLOCKS_PAD + first + SUB] = total
    mixed = jnp.dot(
        mix_ref[0],
        flat_ref[...],
        precision=lax.Precision.HIGHEST,
        preferred_element_type=jnp.float32,
    )
    high = mixed.astype(jnp.bfloat16)
    rest = mixed - high.astype(jnp.float32)
    mid = rest.astype(jnp.bfloat16)
    low = (rest - mid.astype(jnp.float32)).astype(jnp.bfloat16)
    date = lax.broadcasted_iota(jnp.int32, (WIDE, early_ref.shape[1]), 0)
    plus = jnp.where(date == late_ref[...], 1.0, 0.0)
    minus = jnp.where(date == early_ref[...], 1.0, 0.0)
    incidence = (plus - minus).astype(jnp.bfloat16)
    total = jnp.dot(low, incidence, preferred_element_type=jnp.float32)
    total += jnp.dot(mid, incidence, preferred_element_type=jnp.float32)
    total += jnp.dot(high, incidence, preferred_element_type=jnp.float32)
    out_ref[0] = (total * keep_ref[0]).astype(jnp.bfloat16)


def mixing_matrix(near):
    left, right, from_left, from_right = (near[i, :, :, None] for i in range(4))
    place = jnp.arange(SPAN * BLOCKS_PAD, dtype=jnp.int32)
    source = SPAN * (place % BLOCKS_PAD) + place // BLOCKS_PAD
    source = jnp.where((source < DATES) & (place % BLOCKS_PAD < BLOCKS), source, -2)
    source = source.astype(jnp.float32)
    dates = jnp.arange(near.shape[2], dtype=jnp.int32).astype(jnp.float32)
    mix = jnp.where(source == dates[:, None], 1.0, 0.0)[None]
    mix = mix + jnp.where(source == left, from_left, 0.0)
    return mix + jnp.where(source == right, from_right, 0.0)


def build_operators(pair_dates, mask_table, gap_dates, own, width):
    classes, pairs = mask_table.shape
    early, late = pair_dates[:, 0], pair_dates[:, 1]
    lost = jnp.any(
        (gap_dates[:, :, None] == early) | (gap_dates[:, :, None] == late), axis=1
    )
    keep = jnp.where(lost, 0.0, mask_table.astype(jnp.float32))
    padded = round_up(pairs, LANES)
    keep_all = jnp.pad(keep, ((0, round_up(classes, 8) - classes), (0, padded - pairs)))
    early_all = jnp.pad(early[None], ((0, 0), (0, padded - pairs)), constant_values=-1)
    late_all = jnp.pad(late[None], ((0, 0), (0, padded - pairs)), constant_values=-1)
    slots = (2 * LEVELS + 1) * SPAN * SPAN
    extra = keep_all.shape[0] - classes
    gap_all = jnp.pad(gap_dates, ((0, extra), (0, 0)), constant_values=-1)
    coef, near = pl.pallas_call(
        reduction_kernel,
        out_shape=[
            jax.ShapeDtypeStruct((slots, keep_all.shape[0], LANES), jnp.float32),
            jax.ShapeDtypeStruct((4, keep_all.shape[0], WIDE), jnp.float32),
        ],
        compiler_params=pltpu.CompilerParams(vmem_limit_bytes=48 << 20),
        cost_estimate=pl.CostEstimate(flops=1 << 32, bytes_accessed=1 << 20, transcendentals=0),
    )(keep_all, early_all, late_all, gap_all)
    coef = jnp.transpose(coef[:, :classes, :BLOCKS_PAD], (1, 2, 0))
    mix = mixing_matrix(near[:, :classes, :DATES_PAD])
    count = pairs // own[1]
    begin = own[0] * count
    cut = lambda value, fill: jnp.pad(
        lax.dynamic_slice_in_dim(value, begin, count, 1),
        ((0, 0), (0, width - count)),
        constant_values=fill,
    )
    line = pl.BlockSpec((1, width), lambda q: (0, 0))
    return pl.pallas_call(
        inverse_kernel,
        grid=(classes,),
        in_specs=[
            pl.BlockSpec((1, BLOCKS_PAD, slots), lambda q: (q, 0, 0)),
            pl.BlockSpec((1, DATES_PAD, SPAN * BLOCKS_PAD), lambda q: (q, 0, 0)),
            line,
            line,
            pl.BlockSpec((1, 1, width), lambda q: (q, 0, 0)),
        ],
        out_specs=pl.BlockSpec((1, DATES_PAD, width), lambda q: (q, 0, 0)),
        out_shape=jax.ShapeDtypeStruct((classes, DATES_PAD, width), jnp.bfloat16),
        scratch_shapes=[
            pltpu.VMEM((2, SPAN, BLOCKS_PAD + 2 * RIM, WIDE), jnp.float32),
            pltpu.VMEM((SPAN * BLOCKS_PAD, WIDE), jnp.float32),
        ],
        compiler_params=pltpu.CompilerParams(vmem_limit_bytes=48 << 20),
        cost_estimate=pl.CostEstimate(flops=3 << 33, bytes_accessed=4 << 20, transcendentals=0),
    )(coef, mix, cut(early[None], -1), cut(late[None], -1), cut(keep, 0.0)[:, None, :])


def edge_rows(value, axis, width, order=None):
    count, length = lax.axis_size(axis), value.shape[0] if order is None else value.shape[2]
    dim = 0 if order is None else 2
    up = [(i, (i + 1) % count) for i in range(count - 1)]
    down = [(j, i) for i, j in up]
    last = lax.slice_in_dim(value, length - width, length, axis=dim)
    leading = lax.slice_in_dim(value, 0, width, axis=dim)
    if order is not None:
        last, leading = jnp.transpose(last, order), jnp.transpose(leading, order)
    return lax.ppermute(last, axis, up), lax.ppermute(leading, axis, down)


def from_box(boxed, valid):
    power = boxed[0] * boxed[0] + boxed[1] * boxed[1]
    looks = boxed[1] * lax.rsqrt(jnp.maximum(power, 1.0))
    return jnp.where(valid, looks, 0.0).astype(jnp.bfloat16)


def within(pairs, batch, lanes):
    spot = lax.broadcasted_iota(jnp.int32, (batch, lanes), 0) + pl.program_id(0) * batch
    return spot < pairs


def inner_kernel(pairs, planes_ref, band_ref, out_ref, rim_ref, box_ref):
    batch, strip, columns = planes_ref.shape[1:]
    halves = columns // LANES
    for c in range(2):
        along = jnp.dot(
            planes_ref[c].reshape(batch * strip, columns),
            band_ref[...],
            preferred_element_type=jnp.float32,
        )
        for h in range(halves):
            box_ref[c, h] = along[:, h * LANES : (h + 1) * LANES]
    valid = within(pairs, batch, LANES)
    for h in range(halves):
        lanes = slice(h * LANES, (h + 1) * LANES)
        lines = [
            [box_ref[c, h, pl.ds(r, batch, stride=strip), :] for r in range(4)] for c in range(2)
        ]
        for c in range(2):
            near = (lines[c][0] + lines[c][1]) + lines[c][2]
            rim_ref[c, 0, :, lanes] = near
            rim_ref[c, 1, :, lanes] = near + lines[c][3]
        for r in range(2, strip - 2):
            boxed = []
            for c in range(2):
                lines[c].append(box_ref[c, h, pl.ds(r + 2, batch, stride=strip), :])
                a, b, d, e, f = lines[c]
                boxed.append((a + b) + (d + e) + f)
                lines[c].pop(0)
            out_ref[r - 2, :, lanes] = from_box(boxed, valid)
        for c in range(2):
            near = (lines[c][1] + lines[c][2]) + lines[c][3]
            rim_ref[c, 2, :, lanes] = near + lines[c][0]
            rim_ref[c, 3, :, lanes] = near


def outer_kernel(pairs, rim_ref, top_ref, bottom_ref, band_ref, out_ref):
    batch, columns = rim_ref.shape[2:]
    band = band_ref[...]
    valid = within(pairs, batch, columns)
    sums = []
    for c in range(2):
        above = [
            jnp.dot(top_ref[c, i], band, preferred_element_type=jnp.float32) for i in range(2)
        ]
        below = [
            jnp.dot(bottom_ref[c, i], band, preferred_element_type=jnp.float32) for i in range(2)
        ]
        sums.append(
            [
                rim_ref[c, 0] + (above[0] + above[1]),
                rim_ref[c, 1] + above[1],
                rim_ref[c, 2] + below[0],
                rim_ref[c, 3] + (below[0] + below[1]),
            ]
        )
    for r in range(4):
        out_ref[r] = from_box([sums[0][r], sums[1][r]], valid)


def pick_batch(width):
    return 96 if width % 96 == 0 else LANES


def column_band(columns):
    spots = np.arange(columns)
    return jnp.asarray(
        (np.abs(spots[:, None] - spots[None, :]) <= 2).astype(ml_dtypes.bfloat16)
    )


def multilook_inner(interferograms, width):
    pairs, strip, columns = interferograms.shape[1:]
    batch = pick_batch(width)
    return pl.pallas_call(
        functools.partial(inner_kernel, pairs),
        grid=(width // batch,),
        in_specs=[
            pl.BlockSpec((2, batch, strip, columns), lambda j: (0, j, 0, 0)),
            pl.BlockSpec((columns, columns), lambda j: (0, 0)),
        ],
        out_specs=[
            pl.BlockSpec((strip - 4, batch, columns), lambda j: (0, j, 0)),
            pl.BlockSpec((2, 4, batch, columns), lambda j: (0, 0, j, 0)),
        ],
        out_shape=[
            jax.ShapeDtypeStruct((strip - 4, width, columns), jnp.bfloat16),
            jax.ShapeDtypeStruct((2, 4, width, columns), jnp.float32),
        ],
        scratch_shapes=[
            pltpu.VMEM((2, columns // LANES, batch * strip, LANES), jnp.float32)
        ],
        compiler_params=pltpu.CompilerParams(vmem_limit_bytes=40 << 20),
        cost_estimate=pl.CostEstimate(flops=3 << 33, bytes_accessed=24 << 20, transcendentals=0),
    )(interferograms, column_band(columns))


def multilook_outer(rims, top, bottom, pairs):
    width, columns = rims.shape[2:]
    batch = pick_batch(width)
    edge = pl.BlockSpec((2, 2, batch, columns), lambda j: (0, 0, j, 0))
    return pl.pallas_call(
        functools.partial(outer_kernel, pairs),
        grid=(width // batch,),
        in_specs=[
            pl.BlockSpec((2, 4, batch, columns), lambda j: (0, 0, j, 0)),
            edge,
            edge,
            pl.BlockSpec((columns, columns), lambda j: (0, 0)),
        ],
        out_specs=pl.BlockSpec((4, batch, columns), lambda j: (0, j, 0)),
        out_shape=jax.ShapeDtypeStruct((4, width, columns), jnp.bfloat16),
        compiler_params=pltpu.CompilerParams(vmem_limit_bytes=40 << 20),
    )(rims, top, bottom, column_band(columns))


def series_kernel(half_ref, operator_ref, looks_ref, class_ref, out_ref):
    total = jnp.zeros((operator_ref.shape[1], looks_ref.shape[2]), jnp.float32)
    for q in range(operator_ref.shape[0]):
        solved = jnp.dot(operator_ref[q], looks_ref[0], preferred_element_type=jnp.float32)
        total = jnp.where(class_ref[0] == q, solved, total)
    out_ref[0] = total


def invert(operators, looks, pattern_ids, half, rows):
    classes, dates, width = operators.shape
    columns = looks.shape[2]
    return pl.pallas_call(
        series_kernel,
        grid_spec=pltpu.PrefetchScalarGridSpec(
            num_scalar_prefetch=1,
            grid=(rows,),
            in_specs=[
                pl.BlockSpec((classes, dates, width), lambda r, h: (0, 0, 0)),
                pl.BlockSpec((1, width, columns), lambda r, h: (h[0] * rows + r, 0, 0)),
                pl.BlockSpec((1, 1, columns), lambda r, h: (h[0] * rows + r, 0, 0)),
            ],
            out_specs=pl.BlockSpec((1, dates, columns), lambda r, h: (r, 0, 0)),
        ),
        out_shape=jax.ShapeDtypeStruct((rows, dates, columns), jnp.float32),
        compiler_params=pltpu.CompilerParams(vmem_limit_bytes=48 << 20),
        cost_estimate=pl.CostEstimate(
            flops=2 * classes * dates * width * columns * rows,
            bytes_accessed=2 * rows * width * columns + 4 * rows * dates * columns,
            transcendentals=0,
        ),
    )(jnp.reshape(half, (1,)), operators, looks, pattern_ids[:, None, :])


def gauss_taps():
    spots = np.arange(-RADIUS, RADIUS + 1)
    raw = np.exp(-spots * spots / (2.0 * gauss_width * gauss_width))
    return raw / raw.sum()


def screen_kernel(taps, series_ref, before_ref, after_ref, high_ref, low_ref, out_ref):
    rows, tile, columns = series_ref.shape
    lines = [before_ref[i].astype(jnp.float32) for i in range(RADIUS)]
    lines += [series_ref[i] for i in range(rows)]
    lines += [after_ref[i].astype(jnp.float32) for i in range(RADIUS)]
    for r in range(rows):
        total = taps[RADIUS] * lines[r + RADIUS]
        for a in range(RADIUS):
            total += taps[a] * (lines[r + a] + lines[r + 2 * RADIUS - a])
        high = total.astype(jnp.bfloat16)
        low = (total - high.astype(jnp.float32)).astype(jnp.bfloat16)
        screen = jnp.dot(low, high_ref[...], preferred_element_type=jnp.float32)
        screen += jnp.dot(high, low_ref[...], preferred_element_type=jnp.float32)
        screen += jnp.dot(high, high_ref[...], preferred_element_type=jnp.float32)
        out_ref[r] = series_ref[r] - screen


def remove_screen(series, before, after):
    rows, dates, columns = series.shape
    taps = gauss_taps()
    spots = np.arange(columns)
    lag = spots[:, None] - spots[None, :]
    band = np.where(np.abs(lag) <= RADIUS, taps[np.clip(lag, -RADIUS, RADIUS) + RADIUS], 0.0)
    band = band.astype(np.float32)
    high = band.astype(ml_dtypes.bfloat16)
    low = (band - high.astype(np.float32)).astype(ml_dtypes.bfloat16)
    tile = 64
    piece = lambda count: pl.BlockSpec((count, tile, columns), lambda t: (0, t, 0))
    square = pl.BlockSpec((columns, columns), lambda t: (0, 0))
    return pl.pallas_call(
        functools.partial(screen_kernel, [float(x) for x in taps]),
        grid=(-(-dates // tile),),
        in_specs=[piece(rows), piece(RADIUS), piece(RADIUS), square, square],
        out_specs=piece(rows),
        out_shape=jax.ShapeDtypeStruct((rows, DATES, columns), jnp.float32),
        compiler_params=pltpu.CompilerParams(vmem_limit_bytes=48 << 20),
    )(series, before, after, jnp.asarray(high), jnp.asarray(low))


def body(interferograms, pair_dates, mask_table, gap_dates, pattern_ids):
    pairs, strip = interferograms.shape[1:3]
    shares = lax.axis_size("pairs")
    place = lax.axis_index("pairs")
    width = round_up(pairs, LANES)
    top, bottom = edge_rows(interferograms, "rows", 2, (0, 2, 1, 3))
    operators = build_operators(pair_dates, mask_table, gap_dates, (place, shares), width)
    inner_looks, rims = multilook_inner(interferograms, width)
    inner_ids = pattern_ids[2 : strip - 2]
    outer_ids = jnp.concatenate([pattern_ids[:2], pattern_ids[strip - 2 :]])
    across = [(i, 1 - i) for i in range(shares)]
    inner_away = invert(operators, inner_looks, inner_ids, 1 - place, strip // 2 - 2)
    inner_got = lax.ppermute(inner_away, "pairs", across)
    inner_own = invert(operators, inner_looks, inner_ids, place, strip // 2 - 2)
    outer_looks = multilook_outer(rims, top, bottom, pairs)
    outer_away = invert(operators, outer_looks, outer_ids, 1 - place, 2)
    outer_got = lax.ppermute(outer_away, "pairs", across)
    outer_own = invert(operators, outer_looks, outer_ids, place, 2)
    inner = inner_own + inner_got
    outer = outer_own + outer_got
    series = jnp.where(
        place == 0,
        jnp.concatenate([outer, inner]),
        jnp.concatenate([inner, outer]),
    )
    before, after = edge_rows_bf16(series)
    return remove_screen(series, before, after)


def edge_rows_bf16(series):
    return edge_rows(series.astype(jnp.bfloat16), ("rows", "pairs"), RADIUS)


def solution(mesh):
    placed = (
        P(None, "pairs", ("blocks", "rows"), None),
        P(),
        P(),
        P(),
        P(("blocks", "rows"), None),
    )
    return jax.shard_map(
        body,
        mesh=mesh,
        in_specs=placed,
        out_specs=P(("blocks", "rows", "pairs"), None, None),
        check_vma=False,
    )
```

time: 165 us -> 134 us (0.81)
  Pallas kernels: 92.9 us -> 69.5 us
  other arithmetic: 15.7 us -> 5.97 us
  waiting for transfers between devices: 18.6 us -> 22.3 us
  local copies, waits for them, and re-layouts: 22.9 us -> 20.3 us
    pallas_call x4, Pallas kernels: 72.8 us -> 48 us  [the longest x1 25.2 us: build_operators(): pl.pallas_call(inverse_kernel, grid=(classes,), in_specs=[pl.BlockSpec((1...]
    reduce_min x1 -> x0, other arithmetic: 10.2 us -> none  [mixing_matrix(): right = jnp.min(later, axis=2)]
    ppermute x4, waiting for transfers between devices: 18.6 us -> 22.3 us  [edge_rows(): return (lax.ppermute(last, axis, up), lax.ppermute(leading, axis, down))]
    add x1 -> x3, other arithmetic: 0.71 us -> 3.73 us  [the longest x1 1.87 us: body(): inner = inner_own + inner_got]
    convert_element_type x1, other arithmetic: 4.11 us -> 1.77 us  [edge_rows_bf16(): return edge_rows(series.astype(jnp.bfloat16), ('rows', 'pairs'), RADIUS)]
    pallas_call x1, local copies, waits for them, and re-layouts: 2.86 us -> 0.54 us  [build_operators(): pl.pallas_call(reduction_kernel, out_shape=[jax.ShapeDtypeStruct((slots,...]
    pallas_call x2 -> x4, Pallas kernels: 14.7 us -> 16.1 us  [invert(): pl.pallas_call(series_kernel, grid_spec=pltpu.PrefetchScalarGridSpec(num_...]
    unnamed x24 -> x23, local copies, waits for them, and re-layouts: 5.22 us -> 5.22 us
  transfers between devices with their start and end apart: 5 -> 6, of which waited for: 1 -> 2; matrix products, arithmetic and copies ran while one was open for 9% -> 5% of each run, Pallas kernels for 39% -> 48%
where the time goes in v2:
time: 134 us; the launch traced here: 133 us
  Pallas kernels  69.5 us (52%)
  waiting for transfers between devices  22.3 us (17%)
  local copies, waits for them, and re-layouts  20.3 us (15%)
  starting transfers between devices  14.8 us (11%)
  other arithmetic  5.97 us (4%)
    pallas_call x1, Pallas kernels, build_operators(): pl.pallas_call(inverse_kernel, grid=(classes,), in_specs=[pl.BlockSpec((1...  25.2 us
    ppermute x4, waiting for transfers between devices, edge_rows(): return (lax.ppermute(last, axis, up), lax.ppermute(leading, axis, down))  22.3 us
    pallas_call x1, Pallas kernels, multilook_inner(): pl.pallas_call(functools.partial(inner_kernel, pairs), grid=(width // bat...  16.6 us
    pallas_call x4, Pallas kernels, invert(): pl.pallas_call(series_kernel, grid_spec=pltpu.PrefetchScalarGridSpec(num_...  16.1 us
    ppermute x4, starting transfers between devices, edge_rows(): return (lax.ppermute(last, axis, up), lax.ppermute(leading, axis, down))  12.3 us
    transpose x1, local copies, waits for them, and re-layouts, edge_rows(): last, leading = (jnp.transpose(last, order), jnp.transpose(leading, order))  7.96 us
    pallas_call x1, Pallas kernels, remove_screen(): pl.pallas_call(functools.partial(screen_kernel, [float(x) for x in taps])...  5.37 us
    unnamed x23, local copies, waits for them, and re-layouts  5.22 us
  transfers between devices with their start and end apart: 6, of which 2 were waited for; matrix products, arithmetic and copies ran while one was open for 5% of the time, Pallas kernels for 48%

profile of v2, /device:TPU:1, one launch (start us, length us, event | category | flops | bytes accessed | tf_op | source)
XLA Modules:
  0.0 133.2 jit_solution(8765096466823419127)
XLA Ops:
  0.0 8.0 %slice_bitcast_fusion = (bf16[2,2,750,256]{3,1,2,0:T(2,128)(2,1)}, bf16[2,2,750,256]{3,1,2,0:T(2,128)(2,1)}) fusion(bf16[2,750,16,256]{3,2,1,0:T(8,128)(2,1)} %planes_ref.1), kind=kLoop, calls=%fused_computation.2 | loop fusion | bytes 6144000 | tf_op jit(solution)/shard_map/transpose | solution.py:310
  8.0 5.1 %collective-permute-start = (bf16[2,2,750,256]{3,1,2,0:T(2,128)(2,1)}, bf16[2,2,750,256]{3,1,2,0:T(2,128)(2,1)}, u32[]{:S(2)}, u32[]{:S(2)}) collective-permute-start(bf16[2,2,750,256]{3,1,2,0:T(2,128)(2,1)} %get-tuple-element.18), channel_id=1, source_target_pairs={{0,2},{2,4},{4,6},{6,8},{8,10},{10,12},{12,14},{1,3},{3,5},{5,7},{... | collective-permute-start | bytes 4608008 | tf_op jit(solution)/shard_map/ppermute | solution.py:311
  13.1 1.3 collective-permute-start.1
  14.4 0.0 copy-done.9
  14.5 0.0 copy-done.10
  14.5 0.1 copy.18
  14.6 0.3 or_reduce_fusion
  14.9 0.0 copy-done.8
  15.0 2.1 %shard_map.91 = (f32[325,8,128]{2,1,0:T(8,128)S(1)}, f32[4,8,384]{2,1,0:T(8,128)S(1)}) custom-call(f32[8,1536]{1,0:T(8,128)S(1)} %pad.26.keep_ref, s32[1,1536]{1,0:T(1,128)S(1)} %pad.27.early_ref, s32[1,1536]{1,0:T(1,128)S(1)} %pad.28.late_ref, s32[8,30]{1,0:T(8,128)S(1)} %pad.29.gap_ref), custom_call_target="tpu_custom_call" | custom-call | flops 4294967296 | bytes 1048576 | tf_op jit(solution)/shard_map/pallas_call | solution.py:262
  17.1 0.1 constant_dynamic-slice_fusion
  17.2 0.0 copy-start.4
  17.2 0.1 dynamic-slice_bitcast_fusion
  17.3 0.5 copy.19
  17.9 0.2 copy-done.4
  18.1 16.6 %shard_map.93 = (bf16[12,768,256]{2,1,0:T(8,128)(2,1)S(1)}, f32[2,4,768,256]{3,2,1,0:T(8,128)S(1)}) custom-call(bf16[2,750,16,256]{3,2,1,0:T(8,128)(2,1)} %planes_ref.1, bf16[256,256]{1,0:T(8,128)(2,1)S(1)} %copy-done.4), custom_call_target="tpu_custom_call" | custom-call | flops 25769803776 | bytes 25165824 | tf_op jit(solution)/shard_map/pallas_call | solution.py:398
  34.8 2.7 %copy-done = f32[2,4,768,256]{3,2,1,0:T(8,128)} copy-done((f32[2,4,768,256]{3,2,1,0:T(8,128)}, f32[2,4,768,256]{3,2,1,0:T(8,128)S(1)}, u32[]{:S(2)}) %copy-start) | copy-done | bytes 6291480
  37.4 2.2 %copy-done.6 = bf16[12,768,256]{2,1,0:T(8,128)(2,1)} copy-done((bf16[12,768,256]{2,1,0:T(8,128)(2,1)}, bf16[12,768,256]{2,1,0:T(8,128)(2,1)S(1)}, u32[]{:S(2)}) %copy-start.6) | copy-done | bytes 4718616
  39.6 0.1 compare_select_fusion
  39.8 0.7 select_add_fusion.mix_ref
  40.5 0.0 copy-start.7
  40.5 25.2 %shard_map.92.operator_ref = bf16[4,304,768]{2,1,0:T(8,128)(2,1)S(1)} custom-call(f32[4,64,325]{2,1,0:T(8,128)S(1)} %slice_bitcast_fusion.2.coef_ref, f32[4,304,320]{2,1,0:T(8,128)S(1)} %select_add_fusion.mix_ref, s32[1,768]{1,0:T(1,128)S(1)} %pad.30.early_ref, s32[1,768]{1,0:T(1,128)S(1)} %pad.31.late_ref, f32[4,1,768]{2,1,0:T(1,128)S(1)} %broadcast_in_dim.65.keep_ref), custom_call_target="tpu_custom_call" | custom-call | flops 25769803776 | bytes 4194304 | tf_op jit(solution)/shard_map/pallas_call | solution.py:281
  65.7 0.0 copy-done.7
  65.7 7.0 %shard_map.98 = f32[6,304,256]{2,1,0:T(8,128)} custom-call(s32[1]{0:T(128)} %bitcast.12.half_ref, bf16[4,304,768]{2,1,0:T(8,128)(2,1)S(1)} %shard_map.92.operator_ref, bf16[12,768,256]{2,1,0:T(8,128)(2,1)} %copy-done.6, s32[12,1,256]{2,1,0:T(1,128)S(1)} %broadcast_in_dim.67.class_ref), custom_call_target="tpu_custom_call" | custom-call | flops 2868903936 | bytes 4227072 | tf_op jit(solution)/shard_map/pallas_call | solution.py:451
  72.7 1.0 collective-permute-start.3
  73.7 3.7 %collective-permute-done = bf16[2,2,750,256]{3,1,2,0:T(2,128)(2,1)} collective-permute-done((bf16[2,2,750,256]{3,1,2,0:T(2,128)(2,1)}, bf16[2,2,750,256]{3,1,2,0:T(2,128)(2,1)}, u32[]{:S(2)}, u32[]{:S(2)}) %collective-permute-start) | collective-permute-done | bytes 1536032 | tf_op jit(solution)/shard_map/ppermute | solution.py:311
  77.4 1.6 %copy.20.top_ref = bf16[2,2,750,256]{3,2,1,0:T(8,128)(2,1)S(1)} copy(bf16[2,2,750,256]{3,1,2,0:T(2,128)(2,1)} %collective-permute-done) | data formatting | bytes 3072000 | tf_op jit(solution)/shard_map/ppermute | solution.py:311
  79.0 0.0 copy-start.5
  79.0 0.0 collective-permute-done.1
  79.1 1.6 %copy.21.bottom_ref = bf16[2,2,750,256]{3,2,1,0:T(8,128)(2,1)S(1)} copy(bf16[2,2,750,256]{3,1,2,0:T(2,128)(2,1)} %collective-permute-done.1) | data formatting | bytes 3072000 | tf_op jit(solution)/shard_map/ppermute | solution.py:311
  80.7 0.0 copy-done.1
  80.7 0.0 copy-done.5
  80.7 4.1 %shard_map.94.looks_ref = bf16[4,768,256]{2,1,0:T(8,128)(2,1)S(1)} custom-call(f32[2,4,768,256]{3,2,1,0:T(8,128)S(1)} %copy-done.1, bf16[2,2,750,256]{3,2,1,0:T(8,128)(2,1)S(1)} %copy.20.top_ref, bf16[2,2,750,256]{3,2,1,0:T(8,128)(2,1)S(1)} %copy.21.bottom_ref, bf16[256,256]{1,0:T(8,128)(2,1)S(1)} %copy-done.5), custom_call_target="tpu_custom_call" | custom-call | tf_op jit(solution)/shard_map/pallas_call | solution.py:425
  84.8 2.1 %shard_map.96 = f32[2,304,256]{2,1,0:T(8,128)} custom-call(s32[1]{0:T(128)} %bitcast.12.half_ref, bf16[4,304,768]{2,1,0:T(8,128)(2,1)S(1)} %shard_map.92.operator_ref, bf16[4,768,256]{2,1,0:T(8,128)(2,1)S(1)} %shard_map.94.looks_ref, s32[4,1,256]{2,1,0:T(1,128)S(1)} %broadcast_in_dim.66.class_ref), custom_call_target="tpu_custom_call" | custom-call | flops 956301312 | bytes 1409024 | tf_op jit(solution)/shard_map/pallas_call | solution.py:451
  86.9 1.5 %collective-permute-start.2 = (f32[2,304,256]{2,1,0:T(8,128)}, f32[2,304,256]{2,1,0:T(8,128)}, u32[]{:S(2)}, u32[]{:S(2)}) collective-permute-start(f32[2,304,256]{2,1,0:T(8,128)} %shard_map.96), channel_id=1, source_target_pairs={{0,1},{1,0},{2,3},{3,2},{4,5},{5,4},{6,7},{7,6},{8,9},{9,8},{10,11... | collective-permute-start | bytes 1867784 | tf_op jit(solution)/shard_map/ppermute | solution.py:534
  88.4 5.7 %shard_map.97 = f32[6,304,256]{2,1,0:T(8,128)S(1)} custom-call(s32[1]{0:T(128)} %bitcast.half_ref, bf16[4,304,768]{2,1,0:T(8,128)(2,1)S(1)} %shard_map.92.operator_ref, bf16[12,768,256]{2,1,0:T(8,128)(2,1)} %copy-done.6, s32[12,1,256]{2,1,0:T(1,128)S(1)} %broadcast_in_dim.67.class_ref), custom_call_target="tpu_custom_call" | custom-call | flops 2868903936 | bytes 4227072 | tf_op jit(solution)/shard_map/pallas_call | solution.py:451
  94.1 1.3 %shard_map.95 = f32[2,304,256]{2,1,0:T(8,128)S(1)} custom-call(s32[1]{0:T(128)} %bitcast.half_ref, bf16[4,304,768]{2,1,0:T(8,128)(2,1)S(1)} %shard_map.92.operator_ref, bf16[4,768,256]{2,1,0:T(8,128)(2,1)S(1)} %shard_map.94.looks_ref, s32[4,1,256]{2,1,0:T(1,128)S(1)} %broadcast_in_dim.66.class_ref), custom_call_target="tpu_custom_call" | custom-call | flops 956301312 | bytes 1409024 | tf_op jit(solution)/shard_map/pallas_call | solution.py:451
  95.5 0.0 collective-permute-done.3
  95.5 1.9 %add.87 = f32[6,304,256]{2,1,0:T(8,128)S(1)} add(f32[6,304,256]{2,1,0:T(8,128)S(1)} %shard_map.97, f32[6,304,256]{2,1,0:T(8,128)} %collective-permute-done.3) | non-fusion elementwise | flops 466944 | bytes 5603328 | tf_op jit(solution)/shard_map/add | solution.py:536
  97.4 0.0 collective-permute-done.2
  97.4 1.2 add.86
  98.5 1.8 %fusion.8 = (bf16[8,304,256]{2,1,0:T(8,128)(2,1)S(1)}, f32[8,304,256]{2,1,0:T(8,128)}) fusion(f32[2,304,256]{2,1,0:T(8,128)S(1)} %add.86, f32[6,304,256]{2,1,0:T(8,128)S(1)} %add.87, pred[]{:T(512)S(6)} %eq.81), kind=kLoop, calls=%fused_computation.34 | loop fusion | flops 2490368 | bytes 6225921 | tf_op jit(solution)/shard_map/convert_element_type | solution.py:548
  100.3 0.1 fusion.9
  100.4 4.0 %collective-permute-start.4 = (bf16[6,304,256]{2,1,0:T(8,128)(2,1)S(1)}, bf16[6,304,256]{2,1,0:T(8,128)(2,1)S(1)}, u32[]{:S(2)}, u32[]{:S(2)}) collective-permute-start(bf16[6,304,256]{2,1,0:T(8,128)(2,1)S(1)} %get-tuple-element.20), channel_id=1, source_target_pairs={{0,1},{1,2},{2,3},{3,4},{4,5},{5,6},{6,7},{7,8},{8,9},{9,10},{10,1... | collective-permute-start | bytes 2801672 | tf_op jit(solution)/shard_map/ppermute | solution.py:311
  104.4 1.9 %collective-permute-start.5 = (bf16[6,304,256]{2,1,0:T(8,128)(2,1)S(1)}, bf16[6,304,256]{2,1,0:T(8,128)(2,1)S(1)}, u32[]{:S(2)}, u32[]{:S(2)}) collective-permute-start(bf16[6,304,256]{2,1,0:T(8,128)(2,1)S(1)} %get-tuple-element.19), channel_id=1, source_target_pairs={{1,0},{2,1},{3,2},{4,3},{5,4},{6,5},{7,6},{8,7},{9,8},{10,9},{11,1... | collective-permute-start | bytes 2801672 | tf_op jit(solution)/shard_map/ppermute | solution.py:311
  106.4 18.6 %collective-permute-done.4.before_ref = bf16[6,304,256]{2,1,0:T(8,128)(2,1)S(1)} collective-permute-done((bf16[6,304,256]{2,1,0:T(8,128)(2,1)S(1)}, bf16[6,304,256]{2,1,0:T(8,128)(2,1)S(1)}, u32[]{:S(2)}, u32[]{:S(2)}) %collective-permute-start.4) | collective-permute-done | bytes 933920 | tf_op jit(solution)/shard_map/ppermute | solution.py:311
  124.9 0.0 collective-permute-done.5.after_ref
  125.0 5.4 %shard_map.99 = f32[8,300,256]{2,1,0:T(8,128)S(1)} custom-call(f32[8,304,256]{2,1,0:T(8,128)} %get-tuple-element.16.series_ref, bf16[6,304,256]{2,1,0:T(8,128)(2,1)S(1)} %collective-permute-done.4.before_ref, bf16[6,304,256]{2,1,0:T(8,128)(2,1)S(1)} %collective-permute-done.5.after_ref, bf16[256,256]{1,0:T(8,128)(2,1)S(1)} %copy-done.2, ...), custom_call_target="tpu_custom_call" | custom-call | tf_op jit(solution)/shard_map/pallas_call | solution.py:508
  130.3 2.9 %copy.22 = f32[8,300,256]{2,0,1:T(8,128)} copy(f32[8,300,256]{2,1,0:T(8,128)S(1)} %shard_map.99) | data formatting | bytes 4915200 | tf_op jit(solution)/shard_map/pallas_call | solution.py:508
  (29 shorter events, 0.2 us)
Async XLA Ops:
  0.0 14.4 %copy-start.9 = (s32[1500,2]{0,1:T(2,128)S(1)}, s32[1500,2]{0,1:T(2,128)}, u32[]{:S(2)}) copy-start(s32[1500,2]{0,1:T(2,128)} %param.10) | copy-start | bytes 36004
  0.0 14.5 %copy-start.10 = (s32[4,30]{1,0:T(4,128)S(1)}, s32[4,30]{1,0:T(4,128)}, u32[]{:S(2)}) copy-start(s32[4,30]{1,0:T(4,128)} %param.12) | copy-start | bytes 1444
  0.0 14.9 %copy-start.8 = (s32[4,1500]{1,0:T(4,128)S(1)}, s32[4,1500]{1,0:T(4,128)}, u32[]{:S(2)}) copy-start(s32[4,1500]{1,0:T(4,128)} %param.11) | copy-start | bytes 72004
  8.0 69.5 %collective-permute-start = (bf16[2,2,750,256]{3,1,2,0:T(2,128)(2,1)}, bf16[2,2,750,256]{3,1,2,0:T(2,128)(2,1)}, u32[]{:S(2)}, u32[]{:S(2)}) collective-permute-start(bf16[2,2,750,256]{3,1,2,0:T(2,128)(2,1)} %get-tuple-element.18), channel_id=1, source_target_pairs={{0,2},{2,4},{4,6},{6,8},{8,10},{10,12},{12,14},{1,3},{3,5},{5,7},{... | collective-permute-start | bytes 4608008 | tf_op jit(solution)/shard_map/ppermute | solution.py:311
  13.1 65.9 %collective-permute-start.1 = (bf16[2,2,750,256]{3,1,2,0:T(2,128)(2,1)}, bf16[2,2,750,256]{3,1,2,0:T(2,128)(2,1)}, u32[]{:S(2)}, u32[]{:S(2)}) collective-permute-start(bf16[2,2,750,256]{3,1,2,0:T(2,128)(2,1)} %get-tuple-element.17), channel_id=1, source_target_pairs={{2,0},{4,2},{6,4},{8,6},{10,8},{12,10},{14,12},{3,1},{5,3},{7,5},{... | collective-permute-start | bytes 4608008 | tf_op jit(solution)/shard_map/ppermute | solution.py:311
  17.2 0.9 copy-start.4
  34.8 2.7 %copy-start = (f32[2,4,768,256]{3,2,1,0:T(8,128)}, f32[2,4,768,256]{3,2,1,0:T(8,128)S(1)}, u32[]{:S(2)}) copy-start(f32[2,4,768,256]{3,2,1,0:T(8,128)S(1)} %get-tuple-element.11.rim_ref) | copy-start | bytes 18874372
  37.4 2.2 %copy-start.6 = (bf16[12,768,256]{2,1,0:T(8,128)(2,1)}, bf16[12,768,256]{2,1,0:T(8,128)(2,1)S(1)}, u32[]{:S(2)}) copy-start(bf16[12,768,256]{2,1,0:T(8,128)(2,1)S(1)} %get-tuple-element.12.looks_ref) | copy-start | bytes 14155780
  40.5 25.2 %copy-start.7 = (s32[16,256]{1,0:T(8,128)S(1)}, s32[16,256]{1,0:T(8,128)}, u32[]{:S(2)}) copy-start(s32[16,256]{1,0:T(8,128)} %param.13) | copy-start | bytes 49156
  65.7 15.0 %copy-start.1 = (f32[2,4,768,256]{3,2,1,0:T(8,128)S(1)}, f32[2,4,768,256]{3,2,1,0:T(8,128)}, u32[]{:S(2)}) copy-start(f32[2,4,768,256]{3,2,1,0:T(8,128)} %copy-done) | copy-start | bytes 18874372
  72.7 22.8 %collective-permute-start.3 = (f32[6,304,256]{2,1,0:T(8,128)}, f32[6,304,256]{2,1,0:T(8,128)}, u32[]{:S(2)}, u32[]{:S(2)}) collective-permute-start(f32[6,304,256]{2,1,0:T(8,128)} %shard_map.98), channel_id=1, source_target_pairs={{0,1},{1,0},{2,3},{3,2},{4,5},{5,4},{6,7},{7,6},{8,9},{9,8},{10,11... | collective-permute-start | bytes 5603336 | tf_op jit(solution)/shard_map/ppermute | solution.py:530
  79.0 1.7 %copy-start.5 = (bf16[256,256]{1,0:T(8,128)(2,1)S(1)}, bf16[256,256]{1,0:T(8,128)(2,1)}, u32[]{:S(2)}) copy-start(bf16[256,256]{1,0:T(8,128)(2,1)} %constant.73.clone.band_ref) | copy-start | bytes 393220
  86.9 10.5 %collective-permute-start.2 = (f32[2,304,256]{2,1,0:T(8,128)}, f32[2,304,256]{2,1,0:T(8,128)}, u32[]{:S(2)}, u32[]{:S(2)}) collective-permute-start(f32[2,304,256]{2,1,0:T(8,128)} %shard_map.96), channel_id=1, source_target_pairs={{0,1},{1,0},{2,3},{3,2},{4,5},{5,4},{6,7},{7,6},{8,9},{9,8},{10,11... | collective-permute-start | bytes 1867784 | tf_op jit(solution)/shard_map/ppermute | solution.py:534
  100.3 24.6 %copy-start.2 = (bf16[256,256]{1,0:T(8,128)(2,1)S(1)}, bf16[256,256]{1,0:T(8,128)(2,1)}, u32[]{:S(2)}) copy-start(bf16[256,256]{1,0:T(8,128)(2,1)} %constant.74.clone.high_ref) | copy-start | bytes 393220
  100.3 24.6 %copy-start.3 = (bf16[256,256]{1,0:T(8,128)(2,1)S(1)}, bf16[256,256]{1,0:T(8,128)(2,1)}, u32[]{:S(2)}) copy-start(bf16[256,256]{1,0:T(8,128)(2,1)} %constant.75.clone.low_ref) | copy-start | bytes 393220
  100.4 24.5 %collective-permute-start.4 = (bf16[6,304,256]{2,1,0:T(8,128)(2,1)S(1)}, bf16[6,304,256]{2,1,0:T(8,128)(2,1)S(1)}, u32[]{:S(2)}, u32[]{:S(2)}) collective-permute-start(bf16[6,304,256]{2,1,0:T(8,128)(2,1)S(1)} %get-tuple-element.20), channel_id=1, source_target_pairs={{0,1},{1,2},{2,3},{3,4},{4,5},{5,6},{6,7},{7,8},{8,9},{9,10},{10,1... | collective-permute-start | bytes 2801672 | tf_op jit(solution)/shard_map/ppermute | solution.py:311
  104.4 20.5 %collective-permute-start.5 = (bf16[6,304,256]{2,1,0:T(8,128)(2,1)S(1)}, bf16[6,304,256]{2,1,0:T(8,128)(2,1)S(1)}, u32[]{:S(2)}, u32[]{:S(2)}) collective-permute-start(bf16[6,304,256]{2,1,0:T(8,128)(2,1)S(1)} %get-tuple-element.19), channel_id=1, source_target_pairs={{1,0},{2,1},{3,2},{4,3},{5,4},{6,5},{7,6},{8,7},{9,8},{10,9},{11,1... | collective-permute-start | bytes 2801672 | tf_op jit(solution)/shard_map/ppermute | solution.py:311

commit v3 on v2

--- a/solution.py
+++ b/solution.py
@@ -490,7 +490,7 @@
         screen = jnp.dot(low, high_ref[...], preferred_element_type=jnp.float32)
         screen += jnp.dot(high, low_ref[...], preferred_element_type=jnp.float32)
         screen += jnp.dot(high, high_ref[...], preferred_element_type=jnp.float32)
-        out_ref[r] = series_ref[r] - screen
+        out_ref[:, r, :] = series_ref[r] - screen
 
 
 def remove_screen(series, before, after):
@@ -505,14 +505,15 @@
     tile = 64
     piece = lambda count: pl.BlockSpec((count, tile, columns), lambda t: (0, t, 0))
     square = pl.BlockSpec((columns, columns), lambda t: (0, 0))
-    return pl.pallas_call(
+    corrected = pl.pallas_call(
         functools.partial(screen_kernel, [float(x) for x in taps]),
         grid=(-(-dates // tile),),
         in_specs=[piece(rows), piece(RADIUS), piece(RADIUS), square, square],
-        out_specs=piece(rows),
-        out_shape=jax.ShapeDtypeStruct((rows, DATES, columns), jnp.float32),
+        out_specs=pl.BlockSpec((tile, rows, columns), lambda t: (t, 0, 0)),
+        out_shape=jax.ShapeDtypeStruct((DATES, rows, columns), jnp.float32),
         compiler_params=pltpu.CompilerParams(vmem_limit_bytes=48 << 20),
     )(series, before, after, jnp.asarray(high), jnp.asarray(low))
+    return jnp.transpose(corrected, (1, 0, 2))
 
 
 def body(interferograms, pair_dates, mask_table, gap_dates, pattern_ids):
@@ -529,6 +530,7 @@
     inner_away = invert(operators, inner_looks, inner_ids, 1 - place, strip // 2 - 2)
     inner_got = lax.ppermute(inner_away, "pairs", across)
     inner_own = invert(operators, inner_looks, inner_ids, place, strip // 2 - 2)
+    rims, inner_own = lax.optimization_barrier((rims, inner_own))
     outer_looks = multilook_outer(rims, top, bottom, pairs)
     outer_away = invert(operators, outer_looks, outer_ids, 1 - place, 2)
     outer_got = lax.ppermute(outer_away, "pairs", across)

time: 134 us -> 127 us (0.948)
  waiting for transfers between devices: 22.3 us -> 18.6 us
  other arithmetic: 5.97 us -> 4.38 us
  local copies, waits for them, and re-layouts: 20.3 us -> 18.8 us
    ppermute x4, waiting for transfers between devices: 22.3 us -> 18.6 us  [edge_rows(): return (lax.ppermute(last, axis, up), lax.ppermute(leading, axis, down))]
    pallas_call x1 -> x0, local copies, waits for them, and re-layouts: 2.86 us -> none  [remove_screen(): pl.pallas_call(functools.partial(screen_kernel, [float(x) for x in taps])...]
    ppermute x1, starting transfers between devices: 1.55 us -> 0.01 us  [body(): outer_got = lax.ppermute(outer_away, 'pairs', across)]
    convert_element_type x1, other arithmetic: 1.77 us -> 0.3 us  [edge_rows_bf16(): return edge_rows(series.astype(jnp.bfloat16), ('rows', 'pairs'), RADIUS)]
    unnamed x23 -> x29, local copies, waits for them, and re-layouts: 5.22 us -> 6.63 us
  transfers between devices with their start and end apart: 6 -> 6, of which waited for: 2 -> 1; matrix products, arithmetic and copies ran while one was open for 5% -> 6% of each run, Pallas kernels for 48% -> 51%
where the time goes in v3:
time: 127 us; the launch traced here: 126 us
  Pallas kernels  69.4 us (55%)
  local copies, waits for them, and re-layouts  18.8 us (15%)
  waiting for transfers between devices  18.6 us (15%)
  starting transfers between devices  13.9 us (11%)
  other arithmetic  4.38 us (3%)
    pallas_call x1, Pallas kernels, build_operators(): pl.pallas_call(inverse_kernel, grid=(classes,), in_specs=[pl.BlockSpec((1...  25.2 us
    ppermute x4, waiting for transfers between devices, edge_rows(): return (lax.ppermute(last, axis, up), lax.ppermute(leading, axis, down))  18.6 us
    pallas_call x1, Pallas kernels, multilook_inner(): pl.pallas_call(functools.partial(inner_kernel, pairs), grid=(width // bat...  16.6 us
    pallas_call x4, Pallas kernels, invert(): pl.pallas_call(series_kernel, grid_spec=pltpu.PrefetchScalarGridSpec(num_...  16.1 us
    ppermute x4, starting transfers between devices, edge_rows(): return (lax.ppermute(last, axis, up), lax.ppermute(leading, axis, down))  13 us
    transpose x1, local copies, waits for them, and re-layouts, edge_rows(): last, leading = (jnp.transpose(last, order), jnp.transpose(leading, order))  7.93 us
    unnamed x29, local copies, waits for them, and re-layouts  6.63 us
    pallas_call x1, Pallas kernels, remove_screen(): pl.pallas_call(functools.partial(screen_kernel, [float(x) for x in taps])...  5.36 us
  transfers between devices with their start and end apart: 6, of which 1 were waited for; matrix products, arithmetic and copies ran while one was open for 6% of the time, Pallas kernels for 51%

profile of v3, /device:TPU:1, one launch (start us, length us, event | category | flops | bytes accessed | tf_op | source)
XLA Modules:
  0.0 125.5 jit_solution(16769996455778888639)
XLA Ops:
  0.0 7.9 %slice_bitcast_fusion = (bf16[2,2,750,256]{3,1,2,0:T(2,128)(2,1)}, bf16[2,2,750,256]{3,1,2,0:T(2,128)(2,1)}) fusion(bf16[2,750,16,256]{3,2,1,0:T(8,128)(2,1)} %planes_ref.1), kind=kLoop, calls=%fused_computation.2 | loop fusion | bytes 6144000 | tf_op jit(solution)/shard_map/transpose | solution.py:310
  7.9 5.1 %collective-permute-start = (bf16[2,2,750,256]{3,1,2,0:T(2,128)(2,1)}, bf16[2,2,750,256]{3,1,2,0:T(2,128)(2,1)}, u32[]{:S(2)}, u32[]{:S(2)}) collective-permute-start(bf16[2,2,750,256]{3,1,2,0:T(2,128)(2,1)} %get-tuple-element.22), channel_id=1, source_target_pairs={{0,2},{2,4},{4,6},{6,8},{8,10},{10,12},{12,14},{1,3},{3,5},{5,7},{... | collective-permute-start | bytes 4608008 | tf_op jit(solution)/shard_map/ppermute | solution.py:311
  13.1 1.3 %collective-permute-start.1 = (bf16[2,2,750,256]{3,1,2,0:T(2,128)(2,1)}, bf16[2,2,750,256]{3,1,2,0:T(2,128)(2,1)}, u32[]{:S(2)}, u32[]{:S(2)}) collective-permute-start(bf16[2,2,750,256]{3,1,2,0:T(2,128)(2,1)} %get-tuple-element.21), channel_id=1, source_target_pairs={{2,0},{4,2},{6,4},{8,6},{10,8},{12,10},{14,12},{3,1},{5,3},{7,5},{... | collective-permute-start | bytes 4608008 | tf_op jit(solution)/shard_map/ppermute | solution.py:311
  14.4 0.0 copy-done.11
  14.5 0.1 copy.16
  14.6 0.3 or_reduce_fusion
  15.0 2.1 %shard_map.91 = (f32[325,8,128]{2,1,0:T(8,128)S(1)}, f32[4,8,384]{2,1,0:T(8,128)S(1)}) custom-call(f32[8,1536]{1,0:T(8,128)S(1)} %pad.26.keep_ref, s32[1,1536]{1,0:T(1,128)S(1)} %pad.27.early_ref, s32[1,1536]{1,0:T(1,128)S(1)} %pad.28.late_ref, s32[8,30]{1,0:T(8,128)S(1)} %pad.29.gap_ref), custom_call_target="tpu_custom_call" | custom-call | flops 4294967296 | bytes 1048576 | tf_op jit(solution)/shard_map/pallas_call | solution.py:262
  17.1 0.1 constant_dynamic-slice_fusion
  17.2 0.0 copy-start.5
  17.2 0.1 dynamic-slice_bitcast_fusion
  17.3 0.5 copy.17
  17.9 0.2 copy-done.5
  18.1 16.6 %shard_map.93 = (bf16[12,768,256]{2,1,0:T(8,128)(2,1)S(1)}, f32[2,4,768,256]{3,2,1,0:T(8,128)S(1)}) custom-call(bf16[2,750,16,256]{3,2,1,0:T(8,128)(2,1)} %planes_ref.1, bf16[256,256]{1,0:T(8,128)(2,1)S(1)} %copy-done.5), custom_call_target="tpu_custom_call" | custom-call | flops 25769803776 | bytes 25165824 | tf_op jit(solution)/shard_map/pallas_call | solution.py:398
  34.7 2.6 %copy-done = f32[2,4,768,256]{3,2,1,0:T(8,128)} copy-done((f32[2,4,768,256]{3,2,1,0:T(8,128)}, f32[2,4,768,256]{3,2,1,0:T(8,128)S(1)}, u32[]{:S(2)}) %copy-start) | copy-done | bytes 6291480
  37.4 2.2 %copy-done.7 = bf16[12,768,256]{2,1,0:T(8,128)(2,1)} copy-done((bf16[12,768,256]{2,1,0:T(8,128)(2,1)}, bf16[12,768,256]{2,1,0:T(8,128)(2,1)S(1)}, u32[]{:S(2)}) %copy-start.7) | copy-done | bytes 4718616
  39.6 0.1 compare_select_fusion
  39.7 0.7 select_add_fusion.mix_ref
  40.4 0.0 copy-start.8
  40.4 25.2 %shard_map.92.operator_ref = bf16[4,304,768]{2,1,0:T(8,128)(2,1)S(1)} custom-call(f32[4,64,325]{2,1,0:T(8,128)S(1)} %slice_bitcast_fusion.2.coef_ref, f32[4,304,320]{2,1,0:T(8,128)S(1)} %select_add_fusion.mix_ref, s32[1,768]{1,0:T(1,128)S(1)} %pad.30.early_ref, s32[1,768]{1,0:T(1,128)S(1)} %pad.31.late_ref, f32[4,1,768]{2,1,0:T(1,128)S(1)} %broadcast_in_dim.65.keep_ref), custom_call_target="tpu_custom_call" | custom-call | flops 25769803776 | bytes 4194304 | tf_op jit(solution)/shard_map/pallas_call | solution.py:281
  65.7 0.0 slice-start
  65.7 6.8 %shard_map.98 = f32[6,304,256]{2,1,0:T(8,128)} custom-call(s32[1]{0:T(128)} %bitcast.12.half_ref, bf16[4,304,768]{2,1,0:T(8,128)(2,1)S(1)} %shard_map.92.operator_ref, bf16[12,768,256]{2,1,0:T(8,128)(2,1)} %copy-done.7, s32[12,1,256]{2,1,0:T(1,128)S(1)} %broadcast_in_dim.66.class_ref), custom_call_target="tpu_custom_call" | custom-call | flops 2868903936 | bytes 4227072 | tf_op jit(solution)/shard_map/pallas_call | solution.py:451
  72.6 1.0 collective-permute-start.3
  73.5 5.8 %shard_map.94 = f32[6,304,256]{2,1,0:T(8,128)S(1)} custom-call(s32[1]{0:T(128)} %bitcast.half_ref, bf16[4,304,768]{2,1,0:T(8,128)(2,1)S(1)} %shard_map.92.operator_ref, bf16[12,768,256]{2,1,0:T(8,128)(2,1)} %copy-done.7, s32[12,1,256]{2,1,0:T(1,128)S(1)} %broadcast_in_dim.66.class_ref), custom_call_target="tpu_custom_call" | custom-call | flops 2868903936 | bytes 4227072 | tf_op jit(solution)/shard_map/pallas_call | solution.py:451
  79.4 0.0 copy-start.1
  79.4 1.2 copy-done.1
  80.6 0.0 collective-permute-done
  80.6 1.6 %copy.18.top_ref = bf16[2,2,750,256]{3,2,1,0:T(8,128)(2,1)S(1)} copy(bf16[2,2,750,256]{3,1,2,0:T(2,128)(2,1)} %collective-permute-done) | data formatting | bytes 3072000 | tf_op jit(solution)/shard_map/ppermute | solution.py:311
  82.3 0.0 copy-start.6
  82.3 0.0 collective-permute-done.1
  82.3 1.6 %copy.19.bottom_ref = bf16[2,2,750,256]{3,2,1,0:T(8,128)(2,1)S(1)} copy(bf16[2,2,750,256]{3,1,2,0:T(2,128)(2,1)} %collective-permute-done.1) | data formatting | bytes 3072000 | tf_op jit(solution)/shard_map/ppermute | solution.py:311
  84.0 4.1 %shard_map.95.looks_ref = bf16[4,768,256]{2,1,0:T(8,128)(2,1)S(1)} custom-call(f32[2,4,768,256]{3,2,1,0:T(8,128)S(1)} %bitcast.26, bf16[2,2,750,256]{3,2,1,0:T(8,128)(2,1)S(1)} %copy.18.top_ref, bf16[2,2,750,256]{3,2,1,0:T(8,128)(2,1)S(1)} %copy.19.bottom_ref, bf16[256,256]{1,0:T(8,128)(2,1)S(1)} %copy-done.6), custom_call_target="tpu_custom_call" | custom-call | tf_op jit(solution)/shard_map/pallas_call | solution.py:425
  88.1 2.1 %shard_map.97 = f32[2,304,256]{2,1,0:T(8,128)} custom-call(s32[1]{0:T(128)} %bitcast.12.half_ref, bf16[4,304,768]{2,1,0:T(8,128)(2,1)S(1)} %shard_map.92.operator_ref, bf16[4,768,256]{2,1,0:T(8,128)(2,1)S(1)} %shard_map.95.looks_ref, s32[4,1,256]{2,1,0:T(1,128)S(1)} %broadcast_in_dim.67.class_ref), custom_call_target="tpu_custom_call" | custom-call | flops 956301312 | bytes 1409024 | tf_op jit(solution)/shard_map/pallas_call | solution.py:451
  90.1 0.0 collective-permute-start.2
  90.1 1.3 %shard_map.96 = f32[2,304,256]{2,1,0:T(8,128)S(1)} custom-call(s32[1]{0:T(128)} %bitcast.half_ref, bf16[4,304,768]{2,1,0:T(8,128)(2,1)S(1)} %shard_map.92.operator_ref, bf16[4,768,256]{2,1,0:T(8,128)(2,1)S(1)} %shard_map.95.looks_ref, s32[4,1,256]{2,1,0:T(1,128)S(1)} %broadcast_in_dim.67.class_ref), custom_call_target="tpu_custom_call" | custom-call | flops 956301312 | bytes 1409024 | tf_op jit(solution)/shard_map/pallas_call | solution.py:451
  91.5 0.0 collective-permute-done.3
  91.5 0.2 copy-done.2
  91.6 1.8 %add.87 = f32[6,304,256]{2,1,0:T(8,128)S(1)} add(f32[6,304,256]{2,1,0:T(8,128)S(1)} %copy-done.2, f32[6,304,256]{2,1,0:T(8,128)} %collective-permute-done.3) | non-fusion elementwise | flops 466944 | bytes 5603328 | tf_op jit(solution)/shard_map/add | solution.py:538
  93.4 0.0 collective-permute-done.2
  93.4 1.2 add.86
  94.6 0.3 fusion.8
  94.9 0.0 copy-start.3
  94.9 0.0 copy-start.4
  94.9 0.1 fusion.9
  95.0 4.7 %collective-permute-start.4 = (bf16[6,304,256]{2,1,0:T(8,128)(2,1)S(1)}, bf16[6,304,256]{2,1,0:T(8,128)(2,1)S(1)}, u32[]{:S(2)}, u32[]{:S(2)}) collective-permute-start(bf16[6,304,256]{2,1,0:T(8,128)(2,1)S(1)} %get-tuple-element.24), channel_id=1, source_target_pairs={{0,1},{1,2},{2,3},{3,4},{4,5},{5,6},{6,7},{7,8},{8,9},{9,10},{10,1... | collective-permute-start | bytes 2801672 | tf_op jit(solution)/shard_map/ppermute | solution.py:311
  99.7 1.9 %collective-permute-start.5 = (bf16[6,304,256]{2,1,0:T(8,128)(2,1)S(1)}, bf16[6,304,256]{2,1,0:T(8,128)(2,1)S(1)}, u32[]{:S(2)}, u32[]{:S(2)}) collective-permute-start(bf16[6,304,256]{2,1,0:T(8,128)(2,1)S(1)} %get-tuple-element.23), channel_id=1, source_target_pairs={{1,0},{2,1},{3,2},{4,3},{5,4},{6,5},{7,6},{8,7},{9,8},{10,9},{11,1... | collective-permute-start | bytes 2801672 | tf_op jit(solution)/shard_map/ppermute | solution.py:311
  101.6 18.6 %collective-permute-done.4.before_ref = bf16[6,304,256]{2,1,0:T(8,128)(2,1)S(1)} collective-permute-done((bf16[6,304,256]{2,1,0:T(8,128)(2,1)S(1)}, bf16[6,304,256]{2,1,0:T(8,128)(2,1)S(1)}, u32[]{:S(2)}, u32[]{:S(2)}) %collective-permute-start.4) | collective-permute-done | bytes 933920 | tf_op jit(solution)/shard_map/ppermute | solution.py:311
  120.2 0.0 collective-permute-done.5.after_ref
  120.2 5.4 %shard_map.99 = f32[300,8,256]{2,1,0:T(8,128)} custom-call(f32[8,304,256]{2,1,0:T(8,128)S(1)} %get-tuple-element.20.series_ref, bf16[6,304,256]{2,1,0:T(8,128)(2,1)S(1)} %collective-permute-done.4.before_ref, bf16[6,304,256]{2,1,0:T(8,128)(2,1)S(1)} %collective-permute-done.5.after_ref, bf16[256,256]{1,0:T(8,128)(2,1)S(1)} %copy-done.3, ...), custom_call_target="tpu_custom_call" | custom-call | tf_op jit(solution)/shard_map/pallas_call | solution.py:508
  (35 shorter events, 0.2 us)
Async XLA Ops:
  0.0 14.4 %copy-start.10 = (s32[1500,2]{0,1:T(2,128)S(1)}, s32[1500,2]{0,1:T(2,128)}, u32[]{:S(2)}) copy-start(s32[1500,2]{0,1:T(2,128)} %param.10) | copy-start | bytes 36004
  0.0 14.4 %copy-start.11 = (s32[4,30]{1,0:T(4,128)S(1)}, s32[4,30]{1,0:T(4,128)}, u32[]{:S(2)}) copy-start(s32[4,30]{1,0:T(4,128)} %param.12) | copy-start | bytes 1444
  0.0 14.9 %copy-start.9 = (s32[4,1500]{1,0:T(4,128)S(1)}, s32[4,1500]{1,0:T(4,128)}, u32[]{:S(2)}) copy-start(s32[4,1500]{1,0:T(4,128)} %param.11) | copy-start | bytes 72004
  7.9 72.7 %collective-permute-start = (bf16[2,2,750,256]{3,1,2,0:T(2,128)(2,1)}, bf16[2,2,750,256]{3,1,2,0:T(2,128)(2,1)}, u32[]{:S(2)}, u32[]{:S(2)}) collective-permute-start(bf16[2,2,750,256]{3,1,2,0:T(2,128)(2,1)} %get-tuple-element.22), channel_id=1, source_target_pairs={{0,2},{2,4},{4,6},{6,8},{8,10},{10,12},{12,14},{1,3},{3,5},{5,7},{... | collective-permute-start | bytes 4608008 | tf_op jit(solution)/shard_map/ppermute | solution.py:311
  13.1 69.2 %collective-permute-start.1 = (bf16[2,2,750,256]{3,1,2,0:T(2,128)(2,1)}, bf16[2,2,750,256]{3,1,2,0:T(2,128)(2,1)}, u32[]{:S(2)}, u32[]{:S(2)}) collective-permute-start(bf16[2,2,750,256]{3,1,2,0:T(2,128)(2,1)} %get-tuple-element.21), channel_id=1, source_target_pairs={{2,0},{4,2},{6,4},{8,6},{10,8},{12,10},{14,12},{3,1},{5,3},{7,5},{... | collective-permute-start | bytes 4608008 | tf_op jit(solution)/shard_map/ppermute | solution.py:311
  17.2 0.9 copy-start.5
  34.7 2.7 %copy-start = (f32[2,4,768,256]{3,2,1,0:T(8,128)}, f32[2,4,768,256]{3,2,1,0:T(8,128)S(1)}, u32[]{:S(2)}) copy-start(f32[2,4,768,256]{3,2,1,0:T(8,128)S(1)} %get-tuple-element.15.rim_ref) | copy-start | bytes 18874372
  37.4 2.2 %copy-start.7 = (bf16[12,768,256]{2,1,0:T(8,128)(2,1)}, bf16[12,768,256]{2,1,0:T(8,128)(2,1)S(1)}, u32[]{:S(2)}) copy-start(bf16[12,768,256]{2,1,0:T(8,128)(2,1)S(1)} %get-tuple-element.14.looks_ref) | copy-start | bytes 14155780
  40.4 25.2 %copy-start.8 = (s32[16,256]{1,0:T(8,128)S(1)}, s32[16,256]{1,0:T(8,128)}, u32[]{:S(2)}) copy-start(s32[16,256]{1,0:T(8,128)} %param.13) | copy-start | bytes 49156
  65.7 18.2 %slice-start = ((s8[6291456]{0:T(1024)(128)(4,1)}), s8[4194304]{0:T(1024)(128)(4,1)S(1)}, s32[]{:S(2)}) async-start(s8[6291456]{0:T(1024)(128)(4,1)} %bitcast.25), calls=%async_computation | async-start | bytes 8388608
  72.6 18.9 %collective-permute-start.3 = (f32[6,304,256]{2,1,0:T(8,128)}, f32[6,304,256]{2,1,0:T(8,128)}, u32[]{:S(2)}, u32[]{:S(2)}) collective-permute-start(f32[6,304,256]{2,1,0:T(8,128)} %shard_map.98), channel_id=1, source_target_pairs={{0,1},{1,0},{2,3},{3,2},{4,5},{5,4},{6,7},{7,6},{8,9},{9,8},{10,11... | collective-permute-start | bytes 5603336 | tf_op jit(solution)/shard_map/ppermute | solution.py:531
  73.5 10.4 %slice-start.1 = ((s8[6291456]{0:T(1024)(128)(4,1)}), s8[2097152]{0:T(1024)(128)(4,1)S(1)}, s32[]{:S(2)}) async-start(s8[6291456]{0:T(1024)(128)(4,1)} %bitcast.25), calls=%async_computation.1 | async-start | bytes 4194304
  79.4 1.2 copy-start.1
  82.3 1.7 %copy-start.6 = (bf16[256,256]{1,0:T(8,128)(2,1)S(1)}, bf16[256,256]{1,0:T(8,128)(2,1)}, u32[]{:S(2)}) copy-start(bf16[256,256]{1,0:T(8,128)(2,1)} %constant.73.clone.band_ref) | copy-start | bytes 393220
  90.1 3.3 %collective-permute-start.2 = (f32[2,304,256]{2,1,0:T(8,128)}, f32[2,304,256]{2,1,0:T(8,128)}, u32[]{:S(2)}, u32[]{:S(2)}) collective-permute-start(f32[2,304,256]{2,1,0:T(8,128)} %shard_map.97), channel_id=1, source_target_pairs={{0,1},{1,0},{2,3},{3,2},{4,5},{5,4},{6,7},{7,6},{8,9},{9,8},{10,11... | collective-permute-start | bytes 1867784 | tf_op jit(solution)/shard_map/ppermute | solution.py:536
  90.1 1.5 %copy-start.2 = (f32[6,304,256]{2,1,0:T(8,128)S(1)}, f32[6,304,256]{2,1,0:T(8,128)}, u32[]{:S(2)}) copy-start(f32[6,304,256]{2,1,0:T(8,128)} %copy-done.1) | copy-start | bytes 5603332
  94.9 25.3 %copy-start.3 = (bf16[256,256]{1,0:T(8,128)(2,1)S(1)}, bf16[256,256]{1,0:T(8,128)(2,1)}, u32[]{:S(2)}) copy-start(bf16[256,256]{1,0:T(8,128)(2,1)} %constant.74.clone.high_ref) | copy-start | bytes 393220
  94.9 25.3 %copy-start.4 = (bf16[256,256]{1,0:T(8,128)(2,1)S(1)}, bf16[256,256]{1,0:T(8,128)(2,1)}, u32[]{:S(2)}) copy-start(bf16[256,256]{1,0:T(8,128)(2,1)} %constant.75.clone.low_ref) | copy-start | bytes 393220
  95.0 25.2 %collective-permute-start.4 = (bf16[6,304,256]{2,1,0:T(8,128)(2,1)S(1)}, bf16[6,304,256]{2,1,0:T(8,128)(2,1)S(1)}, u32[]{:S(2)}, u32[]{:S(2)}) collective-permute-start(bf16[6,304,256]{2,1,0:T(8,128)(2,1)S(1)} %get-tuple-element.24), channel_id=1, source_target_pairs={{0,1},{1,2},{2,3},{3,4},{4,5},{5,6},{6,7},{7,8},{8,9},{9,10},{10,1... | collective-permute-start | bytes 2801672 | tf_op jit(solution)/shard_map/ppermute | solution.py:311
  99.7 20.5 %collective-permute-start.5 = (bf16[6,304,256]{2,1,0:T(8,128)(2,1)S(1)}, bf16[6,304,256]{2,1,0:T(8,128)(2,1)S(1)}, u32[]{:S(2)}, u32[]{:S(2)}) collective-permute-start(bf16[6,304,256]{2,1,0:T(8,128)(2,1)S(1)} %get-tuple-element.23), channel_id=1, source_target_pairs={{1,0},{2,1},{3,2},{4,3},{5,4},{6,5},{7,6},{8,7},{9,8},{10,9},{11,1... | collective-permute-start | bytes 2801672 | tf_op jit(solution)/shard_map/ppermute | solution.py:311
